TPU v7x, 32 devices: a whole 2x2x4 slice. The times are simulated.
32 devices in a mesh: dom: 8 (over z, y), feat: 4 (over x, core).
Axes of the slice: x: 2, y: 2, z: 4, core: 2. Of those that a mesh axis runs over, the one named last changes fastest.
Arguments:
- latents: bfloat16 [16384, 1024], P('dom', 'feat'), may hold values from -6 to 6
- w_src: bfloat16 [1024, 1024], P(None, 'feat'), may hold values from -0.1875 to 0.1875
- w_dst: bfloat16 [1024, 1024], P(None, 'feat'), may hold values from -0.1875 to 0.1875
- w_edge_out: bfloat16 [1024, 1024], P('feat'), may hold values from -0.1875 to 0.1875
- w_node_in: bfloat16 [2048, 1024], P(None, 'feat'), may hold values from -0.125 to 0.125
- w_node_out: bfloat16 [1024, 1024], P('feat'), may hold values from -0.1875 to 0.1875
- norm_gain: float32 [1024], P('feat'), may hold values from 0.5 to 2
- norm_bias: float32 [1024], P('feat'), may hold values from -3 to 3
- src_tile: int32 [768, 128], P('dom'), may hold values from 0 to 47, as said below
- dst_tile: int32 [8, 96], P('dom'), may hold values from 0 to 15
- src_off: int32 [768, 128], P('dom'), may hold values from 0 to 127
- dst_off: int32 [768, 128], P('dom'), may hold values from 0 to 127
- edge_count: int32 [8], P('dom'), may hold values from 24 to 96, as said below
- send_tiles: int32 [8, 4, 4], P('dom'), may hold values from 0 to 15
Outputs:
- new_latents: bfloat16 [16384, 1024], P('dom', 'feat')
Inputs may be any that keep to these rules, and one draw needn't show every extreme that they name: `src_tile`: in each partition's rows, every edge of edge tile e < 16 has sender tile 16 + e (halo slot e); every edge of edge tiles 16 to 23 has a coarse tile (32 and up), each edge its own; all later edges have sender tiles below 32. `edge_count`: skewed over partitions; some partition has all 96 edge tiles live.
All inputs are finite; a program needn't handle non-finite values.
Results may differ from a plain program's by a relative error of at most 0.013.
Values may be sent and summed in bfloat16 or wider, within the bound.
A program may use at most 128 MiB of HBM per device.

v0:
```python
import jax
import jax.numpy as jnp
from jax import lax
from jax.sharding import PartitionSpec as P

TILE = 128
CT = 2
W = 2


epsilon = 1e-05


def from_behind(block, axis, distance):
    devices = range(lax.axis_size(axis))
    route = [(i - distance, i) for i in devices if i - distance in devices]
    return lax.ppermute(block, axis, route)


def body(
    latents,
    w_src,
    w_dst,
    w_edge_out,
    w_node_in,
    w_node_out,
    norm_gain,
    norm_bias,
    src_tile,
    dst_tile,
    src_off,
    dst_off,
    edge_count,
    send_tiles,
):
    node_rows = latents.shape[0]
    quarter = latents.shape[1]
    full_width = w_src.shape[0]
    shard_piece = lax.all_gather(latents, "feat", axis=1, tiled=True)
    piece_cols = shard_piece.shape[1]
    sender_part = jnp.dot(shard_piece, w_src, preferred_element_type=jnp.float32)
    receiver_part = jnp.dot(shard_piece, w_dst, preferred_element_type=jnp.float32)
    node_part = jnp.dot(
        shard_piece,
        lax.slice_in_dim(w_node_in, 0, piece_cols, axis=0),
        preferred_element_type=jnp.float32,
    )
    node_acc = node_part
    sent_rows = sender_part.astype(jnp.bfloat16)
    received = receiver_part.astype(jnp.bfloat16)
    sender_tiles = sent_rows.reshape(-1, TILE, quarter)
    node_tiles = sender_tiles.shape[0]
    offsets = list(range(-W, 0)) + list(range(1, W + 1))
    halo_parts = []
    for round_index, offset in enumerate(offsets):
        outgoing = sender_tiles[send_tiles[0, round_index]]
        arrived = from_behind(outgoing, "dom", -offset)
        halo_parts.append(arrived.reshape(-1, quarter))
    coarse_rows = lax.all_gather(sender_tiles[:CT], "dom", axis=0, tiled=True).reshape(-1, quarter)
    src_index = (src_tile * TILE + src_off).reshape(-1)
    src_table = jnp.concatenate([sent_rows] + halo_parts + [coarse_rows], 0)
    sources = src_table[src_index].astype(jnp.float32)
    edge_tiles = src_tile.shape[0]
    receiver_of = dst_tile[0]
    within_ids = jnp.arange(TILE, dtype=jnp.int32)
    scatter_table = (dst_off[:, None, :] == within_ids[None, :, None]).astype(jnp.bfloat16)
    recv_tiles = received.reshape(node_tiles, TILE, quarter)[receiver_of]
    targets = jnp.einsum(
        "enm,end->emd", scatter_table, recv_tiles, preferred_element_type=jnp.float32
    )
    live_tiles = (jnp.arange(edge_tiles, dtype=jnp.int32) < edge_count[0]).astype(jnp.float32)
    message = (
        jax.nn.silu(sources.reshape(edge_tiles, TILE, quarter) + targets)
        * live_tiles[:, None, None]
    ).astype(jnp.bfloat16)
    tile_terms = jnp.einsum(
        "enm,emd->end", scatter_table, message, preferred_element_type=jnp.float32
    )
    tile_table = (receiver_of[None, :] == jnp.arange(node_tiles, dtype=jnp.int32)[:, None]).astype(
        jnp.float32
    )
    summed = jnp.einsum(
        "te,end->tnd",
        tile_table,
        tile_terms,
        precision=lax.Precision.HIGHEST,
        preferred_element_type=jnp.float32,
    )
    summed = summed.reshape(node_rows, quarter).astype(jnp.bfloat16)
    partial_agg = jnp.dot(summed, w_edge_out, preferred_element_type=jnp.float32)
    aggregate = lax.psum_scatter(
        partial_agg.astype(jnp.bfloat16), "feat", scatter_dimension=1, tiled=True
    )
    shard_piece = lax.all_gather(aggregate, "feat", axis=1, tiled=True)
    weights_part = lax.dynamic_slice_in_dim(w_node_in, full_width, shard_piece.shape[1], 0)
    node_acc = node_acc + jnp.dot(shard_piece, weights_part, preferred_element_type=jnp.float32)
    hidden = jax.nn.silu(node_acc).astype(jnp.bfloat16)
    out_partial = jnp.dot(hidden, w_node_out, preferred_element_type=jnp.float32)
    mixed_rows = lax.psum_scatter(
        out_partial.astype(jnp.bfloat16), "feat", scatter_dimension=1, tiled=True
    ).astype(jnp.float32)
    sum_values, sum_squares = lax.psum(
        (jnp.sum(mixed_rows, axis=1), jnp.sum(mixed_rows * mixed_rows, axis=1)), "feat"
    )
    average = sum_values[:, None] / full_width
    spread = sum_squares[:, None] / full_width - average * average
    normed = (mixed_rows - average) * lax.rsqrt(spread + epsilon) * norm_gain + norm_bias
    return (latents.astype(jnp.float32) + normed).astype(jnp.bfloat16)


def solution(mesh):
    in_specs = (
        P("dom", "feat"),
        P(None, "feat"),
        P(None, "feat"),
        P("feat", None),
        P(None, "feat"),
        P("feat", None),
        P("feat"),
        P("feat"),
        P("dom", None),
        P("dom", None),
        P("dom", None),
        P("dom", None),
        P("dom"),
        P("dom", None, None),
    )
    out_specs = P("dom", "feat")
    return jax.shard_map(body, mesh=mesh, in_specs=in_specs, out_specs=out_specs, check_vma=False)
```

profile of v0, /device:TPU:0, one launch (start us, length us, event | category | flops | bytes accessed | tf_op | source)
XLA Modules:
  0.0 331.0 jit_solution(15113909619625465780)
XLA Ops:
  10.3 36.3 %all-gather.4.cloned.1.call-done = bf16[2048,1024]{1,0:T(8,128)(2,1)} async-done(((bf16[2048,256]{1,0:T(8,128)(2,1)}), bf16[2048,1024]{1,0:T(8,128)(2,1)}) %all-gather.4.cloned.1.call-update) | async-done | bytes 4194320 | tf_op jit(solution)/shard_map/all_gather | solution.py:39
  46.7 4.4 %constant_dynamic-update-slice_fusion.5 = (bf16[6144,256]{1,0:T(8,128)(2,1)}, bf16[2048,256]{1,0:T(8,128)(2,1)S(1)}) fusion(bf16[2048,1024]{1,0:T(8,128)(2,1)} %all-gather.4.cloned.1.call-done, bf16[1024,256]{1,0:T(8,128)(2,1)S(1)} %copy-done), kind=kOutput, calls=%fused_computation.42 | convolution fusion | flops 1074266112 | bytes 6815744 | tf_op jit(solution)/shard_map/dot_general | solution.py:41
  54.2 4.1 %collective-permute-start = (bf16[4,128,256]{2,1,0:T(8,128)(2,1)S(1)}, bf16[4,128,256]{2,1,0:T(8,128)(2,1)}, u32[]{:S(2)}, u32[]{:S(2)}) collective-permute-start(bf16[4,128,256]{2,1,0:T(8,128)(2,1)S(1)} %gather_fusion), channel_id=1, source_target_pairs={{0,8},{4,12},{8,16},{12,20},{16,24},{20,28},{1,9},{5,13},{9,17},{1... | collective-permute-start | bytes 786440 | tf_op jit(solution)/shard_map/ppermute | solution.py:17
  58.3 3.4 %collective-permute-start.1 = (bf16[4,128,256]{2,1,0:T(8,128)(2,1)S(1)}, bf16[4,128,256]{2,1,0:T(8,128)(2,1)S(1)}, u32[]{:S(2)}, u32[]{:S(2)}) collective-permute-start(bf16[4,128,256]{2,1,0:T(8,128)(2,1)S(1)} %gather_fusion.1), channel_id=1, source_target_pairs={{0,4},{4,8},{8,12},{12,16},{16,20},{20,24},{24,28},{1,5},{5,9},{9,... | collective-permute-start | bytes 786440 | tf_op jit(solution)/shard_map/ppermute | solution.py:17
  61.7 1.3 collective-permute-start.2
  63.0 1.3 collective-permute-start.3
  64.3 3.6 %convolution_convert_fusion.2 = bf16[2048,256]{1,0:T(8,128)(2,1)S(1)} fusion(bf16[2048,1024]{1,0:T(8,128)(2,1)} %all-gather.4.cloned.1.call-done, bf16[1024,256]{1,0:T(8,128)(2,1)} %param.16), kind=kOutput, calls=%fused_computation.20 | convolution fusion | flops 1074266112 | bytes 5767168 | tf_op jit(solution)/shard_map/dot_general | solution.py:42
  67.9 5.9 %gather_fusion.5 = bf16[96,128,256]{2,1,0:T(8,128)(2,1)} fusion(bf16[16,128,256]{2,1,0:T(8,128)(2,1)S(1)} %bitcast.49, s32[1024]{0:T(1024)S(1)} %pad_clamp_fusion), kind=kCustom, calls=%fused_computation.5 | custom fusion | bytes 12583296 | tf_op jit(solution)/shard_map/gather | solution.py:67
  73.8 1.7 constant_dynamic-update-slice_fusion.4
  76.9 3.2 collective-permute-done.3
  80.9 13.6 %all-gather.6.cloned.1.call-done = bf16[16,128,256]{2,1,0:T(8,128)(2,1)} async-done(((bf16[2,128,256]{2,1,0:T(8,128)(2,1)}), bf16[16,128,256]{2,1,0:T(8,128)(2,1)}) %all-gather.6.cloned.1.call-update) | async-done | bytes 1048592 | tf_op jit(solution)/shard_map/all_gather | solution.py:59
  94.5 2.3 constant_dynamic-update-slice_fusion
  96.8 48.5 %gather_fusion.4 = bf16[12288,256]{1,0:T(8,128)(2,1)} fusion(bf16[6144,256]{1,0:T(8,128)(2,1)} %constant_dynamic-update-slice_fusion, s32[12288]{0:T(1024)S(1)} %broadcast_clamp_fusion), kind=kCustom, calls=%fused_computation.4 | custom fusion | bytes 12632064 | tf_op jit(solution)/shard_map/gather | solution.py:62
  145.2 11.9 %fusion.2 = f32[96,128,256]{2,1,0:T(8,128)} fusion(bf16[96,128,256]{2,1,0:T(8,128)(2,1)} %bitcast.51, f32[96]{0:T(128)S(1)} %compare_convert_fusion, bf16[96,128,256]{2,1,0:T(8,128)(2,1)} %gather_fusion.5, s32[96,128]{1,0:T(8,128)S(1)} %copy-done.8), kind=kOutput, calls=%fused_computation.11 | convolution fusion | flops 1638924288 | bytes 25215360 | tf_op jit(solution)/shard_map/enm,emd->end/dot_general | solution.py:76
  157.1 15.5 %fusion.12 = bf16[16,128,256]{2,0,1:T(8,128)(2,1)S(1)} fusion(f32[96,128,256]{2,1,0:T(8,128)} %fusion.2, s32[96]{0:T(128)S(1)} %bitcast.63), kind=kOutput, calls=%fused_computation.29 | convolution fusion | flops 604505600 | bytes 13631872 | tf_op jit(solution)/shard_map/te,end->tnd/dot_general | solution.py:82
  172.9 3.2 convolution_convert_fusion.1
  176.2 43.4 %reduce-scatter.3.cloned.1.call-done = bf16[2048,256]{1,0:T(8,128)(2,1)} async-done(((bf16[2048,1024]{1,0:T(8,128)(2,1)}), bf16[2048,256]{1,0:T(8,128)(2,1)}) %reduce-scatter.3.cloned.1.call-update) | async-done | bytes 1048592 | tf_op jit(solution)/shard_map/reduce_scatter | solution.py:91
  219.9 4.8 %fusion.18 = f32[2048,256]{1,0:T(8,128)} fusion(bf16[2048,1024]{1,0:T(8,128)(2,1)} %all-gather.4.cloned.1.call-done, bf16[2048,256]{1,0:T(8,128)(2,1)S(1)} %copy-done.6), kind=kOutput, calls=%fused_computation.32 | convolution fusion | flops 1073741824 | bytes 6815744 | tf_op jit(solution)/shard_map/dot_general | solution.py:43
  224.7 31.4 %all-gather.8.cloned.1.call-done = bf16[2048,1024]{1,0:T(8,128)(2,1)} async-done(((bf16[2048,256]{1,0:T(8,128)(2,1)}), bf16[2048,1024]{1,0:T(8,128)(2,1)}) %all-gather.8.cloned.1.call-update) | async-done | bytes 4194320 | tf_op jit(solution)/shard_map/all_gather | solution.py:94
  256.2 9.0 %convolution_convert_fusion = bf16[2048,1024]{1,0:T(8,128)(2,1)} fusion(bf16[256,1024]{1,0:T(8,128)(2,1)S(1)} %copy-done.7, f32[2048,256]{1,0:T(8,128)} %fusion.18, bf16[2048,1024]{1,0:T(8,128)(2,1)} %all-gather.8.cloned.1.call-done, bf16[2048,256]{1,0:T(8,128)(2,1)S(1)} %copy-done.6), kind=kOutput, calls=%fused_computation.13 | convolution fusion | flops 2152726528 | bytes 11534336 | tf_op jit(solution)/shard_map/dot_general | solution.py:98
  265.2 44.6 %reduce-scatter.5.cloned.1.call-done = bf16[2048,256]{1,0:T(8,128)(2,1)} async-done(((bf16[2048,1024]{1,0:T(8,128)(2,1)}), bf16[2048,256]{1,0:T(8,128)(2,1)}) %reduce-scatter.5.cloned.1.call-update) | async-done | bytes 1048592 | tf_op jit(solution)/shard_map/reduce_scatter | solution.py:99
  309.8 1.8 convert_reduce_fusion
  311.7 10.1 %all-reduce = (f32[2048]{0:T(1024)S(1)}, f32[2048]{0:T(1024)S(1)}) all-reduce(f32[2048]{0:T(1024)S(1)} %get-tuple-element.6, f32[2048]{0:T(1024)S(1)} %get-tuple-element.5), channel_id=1, replica_groups=mesh['dom'=8,'feat'=4] {'feat'}, use_global_device_ids=true, to_apply=%region_5.6 | all-reduce | flops 4096 | bytes 32768 | tf_op jit(solution)/shard_map/psum | solution.py:102
  321.9 2.6 fusion.10
  (52 shorter events, 9.1 us)
Async XLA Ops:
  6.5 40.1 %copy-start = (bf16[1024,256]{1,0:T(8,128)(2,1)S(1)}, bf16[1024,256]{1,0:T(8,128)(2,1)}, u32[]{:S(2)}) copy-start(bf16[1024,256]{1,0:T(8,128)(2,1)} %param.15) | copy-start | bytes 1572868
  6.5 40.1 %all-gather.4.cloned.1.call-start = ((), (), s32[]{:S(2)}) async-start(), calls=%async_computation.2 | async-start | bytes 5242880 | tf_op jit(solution)/shard_map/all_gather | solution.py:39
  7.3 87.2 %all-gather.6.cloned.1.call-start = ((), (), s32[]{:S(2)}) async-start(), calls=%async_computation.3 | async-start | bytes 1179648 | tf_op jit(solution)/shard_map/all_gather | solution.py:59
  51.8 167.8 %reduce-scatter.3.cloned.1.call-start = ((), (), s32[]{:S(2)}) async-start(), calls=%async_computation.4 | async-start | bytes 5242880 | tf_op jit(solution)/shard_map/reduce_scatter | solution.py:91
  54.2 19.6 %collective-permute-start = (bf16[4,128,256]{2,1,0:T(8,128)(2,1)S(1)}, bf16[4,128,256]{2,1,0:T(8,128)(2,1)}, u32[]{:S(2)}, u32[]{:S(2)}) collective-permute-start(bf16[4,128,256]{2,1,0:T(8,128)(2,1)S(1)} %gather_fusion), channel_id=1, source_target_pairs={{0,8},{4,12},{8,16},{12,20},{16,24},{20,28},{1,9},{5,13},{9,17},{1... | collective-permute-start | bytes 786440 | tf_op jit(solution)/shard_map/ppermute | solution.py:17
  58.3 17.2 %collective-permute-start.1 = (bf16[4,128,256]{2,1,0:T(8,128)(2,1)S(1)}, bf16[4,128,256]{2,1,0:T(8,128)(2,1)S(1)}, u32[]{:S(2)}, u32[]{:S(2)}) collective-permute-start(bf16[4,128,256]{2,1,0:T(8,128)(2,1)S(1)} %gather_fusion.1), channel_id=1, source_target_pairs={{0,4},{4,8},{8,12},{12,16},{16,20},{20,24},{24,28},{1,5},{5,9},{9,... | collective-permute-start | bytes 786440 | tf_op jit(solution)/shard_map/ppermute | solution.py:17
  61.7 14.5 %collective-permute-start.2 = (bf16[4,128,256]{2,1,0:T(8,128)(2,1)S(1)}, bf16[4,128,256]{2,1,0:T(8,128)(2,1)S(1)}, u32[]{:S(2)}, u32[]{:S(2)}) collective-permute-start(bf16[4,128,256]{2,1,0:T(8,128)(2,1)S(1)} %gather_fusion.2), channel_id=1, source_target_pairs={{4,0},{8,4},{12,8},{16,12},{20,16},{24,20},{28,24},{5,1},{9,5},{13... | collective-permute-start | bytes 786440 | tf_op jit(solution)/shard_map/ppermute | solution.py:17
  63.0 17.1 %collective-permute-start.3 = (bf16[4,128,256]{2,1,0:T(8,128)(2,1)S(1)}, bf16[4,128,256]{2,1,0:T(8,128)(2,1)S(1)}, u32[]{:S(2)}, u32[]{:S(2)}) collective-permute-start(bf16[4,128,256]{2,1,0:T(8,128)(2,1)S(1)} %gather_fusion.3), channel_id=1, source_target_pairs={{8,0},{12,4},{16,8},{20,12},{24,16},{28,20},{9,1},{13,5},{17,9},{2... | collective-permute-start | bytes 786440 | tf_op jit(solution)/shard_map/ppermute | solution.py:17
  96.8 48.5 %copy-start.8 = (s32[96,128]{1,0:T(8,128)S(1)}, s32[96,128]{1,0:T(8,128)}, u32[]{:S(2)}) copy-start(s32[96,128]{1,0:T(8,128)} %param.25) | copy-start | bytes 147460
  145.2 11.9 %copy-start.5 = (s32[1,96]{1,0:T(1,128)S(1)}, s32[1,96]{1,0:T(1,128)}, u32[]{:S(2)}) copy-start(s32[1,96]{1,0:T(1,128)} %param.23) | copy-start | bytes 1156
  157.1 15.8 %copy-start.2 = (bf16[256,1024]{1,0:T(8,128)(2,1)S(1)}, bf16[256,1024]{1,0:T(8,128)(2,1)}, u32[]{:S(2)}) copy-start(bf16[256,1024]{1,0:T(8,128)(2,1)} %param.17) | copy-start | bytes 1572868
  176.2 43.7 %copy-start.6 = (bf16[2048,256]{1,0:T(8,128)(2,1)S(1)}, bf16[2048,256]{1,0:T(8,128)(2,1)}, u32[]{:S(2)}) copy-start(bf16[2048,256]{1,0:T(8,128)(2,1)} %param.18) | copy-start | bytes 3145732
  176.2 80.0 %all-gather.8.cloned.1.call-start = ((), (), s32[]{:S(2)}) async-start(), calls=%async_computation.5 | async-start | bytes 5242880 | tf_op jit(solution)/shard_map/all_gather | solution.py:94
  219.6 36.6 %copy-start.7 = (bf16[256,1024]{1,0:T(8,128)(2,1)S(1)}, bf16[256,1024]{1,0:T(8,128)(2,1)}, u32[]{:S(2)}) copy-start(bf16[256,1024]{1,0:T(8,128)(2,1)} %param.19) | copy-start | bytes 1572868
  219.6 90.2 %reduce-scatter.5.cloned.1.call-start = ((), (), s32[]{:S(2)}) async-start(), calls=%async_computation.6 | async-start | bytes 5242880 | tf_op jit(solution)/shard_map/reduce_scatter | solution.py:99
  265.2 56.7 %copy-start.1 = (bf16[2048,256]{1,0:T(8,128)(2,1)S(1)}, bf16[2048,256]{1,0:T(8,128)(2,1)}, u32[]{:S(2)}) copy-start(bf16[2048,256]{1,0:T(8,128)(2,1)} %param.14) | copy-start | bytes 3145732
  265.2 56.7 %copy-start.3 = (f32[256]{0:T(256)S(1)}, f32[256]{0:T(256)}, u32[]{:S(2)}) copy-start(f32[256]{0:T(256)} %param.21) | copy-start | bytes 3076
  265.2 56.7 %copy-start.4 = (f32[256]{0:T(256)S(1)}, f32[256]{0:T(256)}, u32[]{:S(2)}) copy-start(f32[256]{0:T(256)} %param.20) | copy-start | bytes 3076
Sparse Core Ops, SparseCore 0:
  8.9 37.7 all-gather.3
  51.9 42.5 all-gather.5
  176.3 43.2 reduce-scatter.2
  221.1 35.0 all-gather.7
  265.3 44.4 reduce-scatter.4
where the time goes:
time: 331 us
  waiting for transfers between devices  173 us (52%)
  local copies, waits for them, and re-layouts  63.8 us (19%)
  matrix products  52.4 us (16%)
  between operations  14 us (4%)
  starting transfers between devices  10.5 us (3%)
  blocking collectives  10.1 us (3%)
  other arithmetic  6.83 us (2%)
    gather x1, local copies, waits for them, and re-layouts, body(): sources = src_table[src_index].astype(jnp.float32)  48.5 us
    reduce_scatter x1, waiting for transfers between devices, body(): lax.psum_scatter(out_partial.astype(jnp.bfloat16), 'feat', scatter_dimens...  44.6 us
    reduce_scatter x1, waiting for transfers between devices, body(): lax.psum_scatter(partial_agg.astype(jnp.bfloat16), 'feat', scatter_dimens...  43.4 us
    all_gather x1, waiting for transfers between devices, body(): shard_piece = lax.all_gather(latents, 'feat', axis=1, tiled=True)  36.3 us
    all_gather x1, waiting for transfers between devices, body(): shard_piece = lax.all_gather(aggregate, 'feat', axis=1, tiled=True)  31.4 us
    dot_general x1, matrix products, body(): jnp.einsum('te,end->tnd', tile_table, tile_terms, precision=lax.Precision...  15.5 us
    all_gather x1, waiting for transfers between devices, body(): lax.all_gather(sender_tiles[:CT], 'dom', axis=0, tiled=True)  13.6 us
    dot_general x1, matrix products, body(): jnp.einsum('enm,emd->end', scatter_table, message, preferred_element_type...  11.9 us
  transfers between devices with their start and end apart: 9, of which 6 were waited for; matrix products, arithmetic and copies ran while one was open for 7% of the time, Pallas kernels for 0%

commit v1 on v0

v1 whole, which is shorter than its diff:
```python
import functools

import jax
import jax.numpy as jnp
from jax import lax
from jax.experimental import pallas as pl
from jax.experimental.pallas import tpu as pltpu
from jax.sharding import PartitionSpec as P

TILE = 128
CT = 2
W = 2
MESH = pl.DeviceIdType.MESH
BF = jnp.bfloat16
F32 = jnp.float32
MIB = 1 << 20

epsilon = 1e-05


def swish(v):
    half = 0.5 * v
    return half + half * jnp.tanh(half)


def project_kernel(
    lat_ref,
    ws_ref,
    wd_ref,
    st_ref,
    table_ref,
    recv_ref,
    rows_ref,
    parts,
    held,
    halo,
    own_sem,
    a1_send,
    a1_recv,
    a2_send,
    a2_recv,
    b_send,
    b_recv,
    c_send,
    c_recv,
    h_send,
    h_recv,
):
    nf, nodes, width = parts.shape
    nd = lax.axis_size("dom")
    feat = lax.axis_index("feat")
    dom = lax.axis_index("dom")
    rounds, batch = st_ref.shape[1:]
    chunks = a1_send.shape[0]
    step = nodes // chunks
    x, core = feat // 2, feat % 2
    near = x * 2 + (1 - core)
    far = (1 - x) * 2 + core
    offsets = list(range(-W, 0)) + list(range(1, W + 1))
    coarse_at = nodes + rounds * batch * TILE
    coarse_rows = CT * TILE

    barrier = pltpu.get_barrier_semaphore()
    for peer in (near, far):
        pl.semaphore_signal(barrier, inc=1, device_id={"feat": peer}, device_id_type=MESH)
    for k in range(1, nd):
        pl.semaphore_signal(
            barrier, inc=1, device_id={"dom": lax.rem(dom + k, nd)}, device_id_type=MESH
        )
    pl.semaphore_wait(barrier, nd + 1)

    def first(c, peer, send, recv):
        rows = pl.ds(c * step, step)
        return pltpu.make_async_remote_copy(
            src_ref=lat_ref.at[rows],
            dst_ref=parts.at[feat, rows],
            send_sem=send.at[c],
            recv_sem=recv.at[c],
            device_id={"feat": peer},
            device_id_type=MESH,
        )

    to_far = [first(c, far, a2_send, a2_recv) for c in range(chunks)]
    to_near = [first(c, near, a1_send, a1_recv) for c in range(chunks)]
    onward = []
    for c in range(chunks):
        rows = pl.ds(c * step, step)
        onward.append(
            pltpu.make_async_remote_copy(
                src_ref=parts.at[far, rows],
                dst_ref=parts.at[far, rows],
                send_sem=b_send.at[c],
                recv_sem=b_recv.at[c],
                device_id={"feat": near},
                device_id_type=MESH,
            )
        )
    own = pltpu.make_async_copy(lat_ref, parts.at[feat], own_sem)
    for c in range(chunks):
        to_far[c].start()
    own.start()
    for c in range(chunks):
        to_near[c].start()
    own.wait()

    coarse = []
    for k in range(1, nd):
        coarse.append(
            pltpu.make_async_remote_copy(
                src_ref=table_ref.at[pl.ds(0, coarse_rows)],
                dst_ref=table_ref.at[pl.ds(coarse_at + dom * coarse_rows, coarse_rows)],
                send_sem=c_send.at[k],
                recv_sem=c_recv.at[k],
                device_id={"dom": lax.rem(dom + k, nd)},
                device_id_type=MESH,
            )
        )

    def project(c):
        to_near[c].wait_recv()
        onward[c].wait_recv()
        rows = pl.ds(c * step, step)
        lat = jnp.concatenate([parts[f, rows, :] for f in range(nf)], axis=1)
        sent = jnp.dot(lat, ws_ref[...], preferred_element_type=F32).astype(BF)
        tiles = step // TILE
        held[pl.ds(c * tiles, tiles)] = sent.reshape(tiles, TILE, width)
        table_ref[rows, :] = sent
        recv_ref[rows, :] = jnp.dot(lat, wd_ref[...], preferred_element_type=F32).astype(BF)
        if c == 0:
            for copy in coarse:
                copy.start()
            table_ref[pl.ds(coarse_at + dom * coarse_rows, coarse_rows), :] = sent[:coarse_rows]

    for c in range(chunks):
        to_far[c].wait_recv()
        onward[c].start()
        if c > 0:
            project(c - 1)
    project(chunks - 1)

    spread = []
    for r, offset in enumerate(offsets):
        base = nodes + r * batch * TILE
        for b in range(batch):
            tile = st_ref[0, r, b]
            halo[r, pl.ds(b * TILE, TILE), :] = held[tile]
        target = dom - offset
        copy = pltpu.make_async_remote_copy(
            src_ref=halo.at[r],
            dst_ref=table_ref.at[pl.ds(base, batch * TILE)],
            send_sem=h_send.at[r],
            recv_sem=h_recv.at[r],
            device_id={"dom": lax.rem(target + nd, nd)},
            device_id_type=MESH,
        )
        source = dom + offset
        sends = target >= 0 if offset > 0 else target < nd
        gets = source >= 0 if offset < 0 else source < nd
        lacks = source < 0 if offset < 0 else source >= nd
        spread.append((copy, sends, gets))

        @pl.when(sends)
        def _(copy=copy):
            copy.start()

        @pl.when(lacks)
        def _(base=base):
            table_ref[pl.ds(base, batch * TILE), :] = jnp.zeros((batch * TILE, width), BF)

    share = nodes // nf
    for f in range(nf):
        rows_ref[:, f * width : (f + 1) * width] = parts[f, pl.ds(feat * share, share), :]

    for copy, sends, gets in spread:

        @pl.when(sends)
        def _(copy=copy):
            copy.wait_send()

        @pl.when(gets)
        def _(copy=copy):
            copy.wait_recv()

    for copy in coarse:
        copy.wait_send()
        copy.wait_recv()
    for c in range(chunks):
        to_far[c].wait_send()
        to_near[c].wait_send()
        onward[c].wait_send()


UNROLL = 4


def edge_kernel(
    idx_ref, dst_tile_ref, count_ref, off_ref, table_ref, recv_ref, out_ref, wide, acc, *slots
):
    rows, width = table_ref.shape
    half = width // 2
    block = 8 * TILE

    @pl.loop(0, rows // block)
    def _(i):
        part = table_ref[pl.ds(pl.multiple_of(i * block, block), block), :].astype(F32)
        at = pl.multiple_of(i * (2 * block), 2 * block)
        wide[pl.ds(at, block, stride=2), :] = part[:, :half]
        wide[pl.ds(at + 1, block, stride=2), :] = part[:, half:]

    acc[...] = jnp.zeros_like(acc)
    ids = lax.broadcasted_iota(jnp.int32, (TILE, TILE), 0)
    count = count_ref[0]

    @pl.loop(0, (count + UNROLL - 1) // UNROLL)
    def _(i):
        for u in range(UNROLL):
            e = i * UNROLL + u
            slot = slots[u]
            for n in range(TILE):
                slot[pl.ds(2 * n, 2), :] = wide[pl.ds(idx_ref[e, n], 2), :]
        for u in range(UNROLL):
            e = i * UNROLL + u
            slot = slots[u]
            live = (e < count).astype(F32)
            node = pl.ds(pl.multiple_of(dst_tile_ref[0, e] * TILE, TILE), TILE)
            scatter = (ids == off_ref[pl.ds(e, 1), :]).astype(F32).astype(BF)
            target = lax.dot_general(
                scatter, recv_ref[node, :], (((0,), (0,)), ((), ())), preferred_element_type=F32
            )
            source = jnp.concatenate(
                [slot[pl.ds(0, TILE, stride=2), :], slot[pl.ds(1, TILE, stride=2), :]], axis=1
            )
            message = (swish(source + target) * live).astype(BF)
            acc[node, :] += jnp.dot(scatter, message, preferred_element_type=F32)

    out_ref[...] = acc[...].astype(BF)


def node_kernel(
    summed_ref,
    rows_ref,
    we_hbm,
    wi_hbm,
    wo_hbm,
    gain_ref,
    bias_ref,
    out_ref,
    we,
    wi,
    wo,
    taken,
    given,
    load_sem,
    keep_sem,
    in_send,
    in_recv,
    out_send,
    out_recv,
):
    nf, share, width = taken.shape
    full = nf * width
    feat = lax.axis_index("feat")
    chunks = keep_sem.shape[0]
    step = share // chunks

    barrier = pltpu.get_barrier_semaphore()
    for k in range(1, nf):
        pl.semaphore_signal(
            barrier, inc=1, device_id={"feat": lax.rem(feat + k, nf)}, device_id_type=MESH
        )
    loads = [
        pltpu.make_async_copy(src, dst, load_sem.at[i])
        for i, (src, dst) in enumerate(((wi_hbm, wi), (we_hbm, we), (wo_hbm, wo)))
    ]
    pl.semaphore_wait(barrier, nf - 1)

    ins = {}
    for c in range(chunks):
        for k in (2, 1, 3):
            peer = lax.rem(feat + k, nf)
            ins[c, k] = pltpu.make_async_remote_copy(
                src_ref=summed_ref.at[pl.ds(peer * share + c * step, step)],
                dst_ref=taken.at[feat, pl.ds(c * step, step)],
                send_sem=in_send.at[c, k],
                recv_sem=in_recv.at[c, k],
                device_id={"feat": peer},
                device_id_type=MESH,
            )
            ins[c, k].start()
    for load in loads:
        load.start()
    taken[feat] = summed_ref[pl.ds(feat * share, share), :]
    for load in loads:
        load.wait()

    outs = []
    keeps = []
    for c in range(chunks):
        rows = pl.ds(c * step, step)
        lat = rows_ref[rows, :]
        first = [
            jnp.dot(lat, wi[f, :full, :], preferred_element_type=F32) for f in range(nf)
        ]
        for k in (2, 1, 3):
            ins[c, k].wait_recv()
        total = jnp.zeros((step, full), F32)
        for f in range(nf):
            term = jnp.dot(
                taken[f, rows, :], we[f * width : (f + 1) * width, :], preferred_element_type=F32
            )
            total = total + term.astype(BF).astype(F32)
        aggregate = total.astype(BF)
        update = jnp.zeros((step, full), F32)
        for f in range(nf):
            pre = first[f] + jnp.dot(aggregate, wi[f, full:, :], preferred_element_type=F32)
            hidden = swish(pre).astype(BF)
            term = jnp.dot(hidden, wo[f * width : (f + 1) * width, :], preferred_element_type=F32)
            update = update + term.astype(BF).astype(F32)
        average = jnp.sum(update, axis=1, keepdims=True) / full
        spread = jnp.sum(update * update, axis=1, keepdims=True) / full - average * average
        normed = (update - average) * lax.rsqrt(spread + epsilon) * gain_ref[...] + bias_ref[...]
        result = (lat.astype(F32) + normed).astype(BF)
        for f in range(nf):
            given[f, rows, :] = result[:, f * width : (f + 1) * width]
        place = pl.ds(feat * share + c * step, step)
        for k in (2, 1, 3):
            peer = lax.rem(feat + k, nf)
            copy = pltpu.make_async_remote_copy(
                src_ref=given.at[peer, rows],
                dst_ref=out_ref.at[place],
                send_sem=out_send.at[c, k],
                recv_sem=out_recv.at[c, k],
                device_id={"feat": peer},
                device_id_type=MESH,
            )
            copy.start()
            outs.append(copy)
        keep = pltpu.make_async_copy(given.at[feat, rows], out_ref.at[place], keep_sem.at[c])
        keep.start()
        keeps.append(keep)
    for keep in keeps:
        keep.wait()
    for copy in outs:
        copy.wait_send()
        copy.wait_recv()
    for copy in ins.values():
        copy.wait_send()


def vmem():
    return pl.BlockSpec(memory_space=pltpu.VMEM)


def smem():
    return pl.BlockSpec(memory_space=pltpu.SMEM)


def hbm():
    return pl.BlockSpec(memory_space=pl.ANY)


def dma(*shape):
    return pltpu.SemaphoreType.DMA(shape)


def body(
    latents,
    w_src,
    w_dst,
    w_edge_out,
    w_node_in,
    w_node_out,
    norm_gain,
    norm_bias,
    src_tile,
    dst_tile,
    src_off,
    dst_off,
    edge_count,
    send_tiles,
):
    nodes, width = latents.shape
    full = w_src.shape[0]
    nf = lax.axis_size("feat")
    nd = lax.axis_size("dom")
    rounds, batch = send_tiles.shape[1:]
    share = nodes // nf
    table_rows = nodes + rounds * batch * TILE + nd * CT * TILE
    edge_tiles = src_tile.shape[0]
    chunks = 8

    we = lax.all_gather(w_edge_out, "feat", axis=0, tiled=True)
    wi = lax.all_gather(w_node_in, "feat", axis=0)
    wo = lax.all_gather(w_node_out, "feat", axis=0, tiled=True)
    norm = lax.all_gather(jnp.stack([norm_gain, norm_bias]), "feat", axis=1, tiled=True)

    table, received, rows = pl.pallas_call(
        project_kernel,
        out_shape=(
            jax.ShapeDtypeStruct((table_rows, width), BF),
            jax.ShapeDtypeStruct((nodes, width), BF),
            jax.ShapeDtypeStruct((share, full), BF),
        ),
        in_specs=[hbm(), vmem(), vmem(), smem()],
        out_specs=(vmem(), vmem(), vmem()),
        scratch_shapes=[
            pltpu.VMEM((nf, nodes, width), BF),
            pltpu.VMEM((nodes // TILE, TILE, width), BF),
            pltpu.VMEM((rounds, batch * TILE, width), BF),
            pltpu.SemaphoreType.DMA,
            *[dma(chunks) for _ in range(6)],
            dma(nd),
            dma(nd),
            dma(rounds),
            dma(rounds),
        ],
        compiler_params=pltpu.CompilerParams(
            collective_id=0, has_side_effects=True, vmem_limit_bytes=40 * MIB
        ),
        cost_estimate=pl.CostEstimate(
            flops=4 * nodes * full * width, bytes_accessed=100 * MIB, transcendentals=0
        ),
        name="project",
    )(latents, w_src, w_dst, send_tiles)

    index = (src_tile * TILE + src_off) * 2
    summed = pl.pallas_call(
        edge_kernel,
        out_shape=jax.ShapeDtypeStruct((nodes, width), BF),
        in_specs=[smem(), smem(), smem(), vmem(), vmem(), vmem()],
        out_specs=vmem(),
        scratch_shapes=[
            pltpu.VMEM((2 * table_rows, width // 2), F32),
            pltpu.VMEM((nodes, width), F32),
            *[pltpu.VMEM((2 * TILE, width // 2), F32) for _ in range(UNROLL)],
        ],
        compiler_params=pltpu.CompilerParams(vmem_limit_bytes=56 * MIB),
        cost_estimate=pl.CostEstimate(
            flops=4 * edge_tiles * TILE * TILE * width,
            bytes_accessed=100 * MIB,
            transcendentals=edge_tiles * TILE * width,
        ),
        name="edges",
    )(index, dst_tile, edge_count, dst_off, table, received)

    return pl.pallas_call(
        node_kernel,
        out_shape=jax.ShapeDtypeStruct((nodes, width), BF),
        in_specs=[vmem(), vmem(), hbm(), hbm(), hbm(), vmem(), vmem()],
        out_specs=hbm(),
        scratch_shapes=[
            pltpu.VMEM((full, full), BF),
            pltpu.VMEM((nf, 2 * full, width), BF),
            pltpu.VMEM((full, full), BF),
            pltpu.VMEM((nf, share, width), BF),
            pltpu.VMEM((nf, share, width), BF),
            dma(3),
            dma(4),
            dma(4, nf),
            dma(4, nf),
            dma(4, nf),
            dma(4, nf),
        ],
        compiler_params=pltpu.CompilerParams(
            collective_id=1, has_side_effects=True, vmem_limit_bytes=40 * MIB
        ),
        cost_estimate=pl.CostEstimate(
            flops=8 * share * full * full, bytes_accessed=60 * MIB, transcendentals=share * full
        ),
        name="nodes",
    )(summed, rows, we, wi, wo, norm[0:1], norm[1:2])


def solution(mesh):
    in_specs = (
        P("dom", "feat"),
        P(None, "feat"),
        P(None, "feat"),
        P("feat", None),
        P(None, "feat"),
        P("feat", None),
        P("feat"),
        P("feat"),
        P("dom", None),
        P("dom", None),
        P("dom", None),
        P("dom", None),
        P("dom"),
        P("dom", None, None),
    )
    out_specs = P("dom", "feat")
    return jax.shard_map(body, mesh=mesh, in_specs=in_specs, out_specs=out_specs, check_vma=False)
```

time: 331 us -> 144 us (0.44)
  waiting for transfers between devices: 173 us -> 19.3 us
  Pallas kernels: 0 us -> 88.9 us
  matrix products: 52.4 us -> 0 us
  local copies, waits for them, and re-layouts: 63.8 us -> 14.3 us
  starting transfers between devices: 10.5 us -> 0.08 us
  other arithmetic: 6.83 us -> 1.34 us
  blocking collectives: 10.1 us -> 6.1 us
    pallas_call x0 -> x3, Pallas kernels: none -> 88.9 us  [the longest x1 52.3 us: body(): pl.pallas_call(project_kernel, out_shape=(jax.ShapeDtypeStruct((table_row...]
    reduce_scatter x2 -> x0, waiting for transfers between devices: 88 us -> none  [the longest x1 44.6 us: body(): lax.psum_scatter(out_partial.astype(jnp.bfloat16), 'feat', scatter_dimens...]
    all_gather x3, waiting for transfers between devices: 81.4 us -> 17.2 us  [the longest x1 17.2 us: body(): wi = lax.all_gather(w_node_in, 'feat', axis=0)]
    gather x6 -> x0, local copies, waits for them, and re-layouts: 56.6 us -> none  [the longest x1 48.5 us: body(): sources = src_table[src_index].astype(jnp.float32)]
    dot_general x7 -> x0, matrix products: 52.4 us -> none  [the longest x1 15.5 us: body(): jnp.einsum('te,end->tnd', tile_table, tile_terms, precision=lax.Precision...]
    unnamed x22 -> x25, local copies, waits for them, and re-layouts: 3.87 us -> 14.3 us
    psum x1 -> x0, blocking collectives: 10.1 us -> none  [body(): lax.psum((jnp.sum(mixed_rows, axis=1), jnp.sum(mixed_rows * mixed_rows, a...]
    ppermute x4 -> x0, starting transfers between devices: 10.1 us -> none  [from_behind(): return lax.ppermute(block, axis, route)]
  transfers between devices with their start and end apart: 9 -> 3, of which waited for: 6 -> 1; matrix products, arithmetic and copies ran while one was open for 7% -> 1% of each run, Pallas kernels for 0% -> 44%
where the time goes in v1:
time: 144 us
  Pallas kernels  88.9 us (62%)
  waiting for transfers between devices  19.3 us (13%)
  local copies, waits for them, and re-layouts  14.3 us (10%)
  between operations  13.8 us (10%)
  blocking collectives  6.1 us (4%)
    pallas_call x1, Pallas kernels, body(): pl.pallas_call(project_kernel, out_shape=(jax.ShapeDtypeStruct((table_row...  52.3 us
    pallas_call x1, Pallas kernels, body(): pl.pallas_call(node_kernel, out_shape=jax.ShapeDtypeStruct((nodes, width)...  25.7 us
    all_gather x1, waiting for transfers between devices, body(): wi = lax.all_gather(w_node_in, 'feat', axis=0)  17.2 us
    unnamed x25, local copies, waits for them, and re-layouts  14.3 us
    pallas_call x1, Pallas kernels, body(): pl.pallas_call(edge_kernel, out_shape=jax.ShapeDtypeStruct((nodes, width)...  10.9 us
    all_gather x1, blocking collectives, body(): lax.all_gather(jnp.stack([norm_gain, norm_bias]), 'feat', axis=1, tiled=T...  6.1 us
  transfers between devices with their start and end apart: 3, of which 1 were waited for; matrix products, arithmetic and copies ran while one was open for 1% of the time, Pallas kernels for 44%

profile of v1, /device:TPU:0, one launch (start us, length us, event | category | flops | bytes accessed | tf_op | source)
XLA Modules:
  0.0 143.8 jit_solution(16685174602038642981)
XLA Ops:
  6.5 0.7 all-gather.5.cloned.1.call-update
  7.3 0.0 all-gather.7.cloned.1.call-start
  7.3 0.7 all-gather.7.cloned.1.call-update
  8.0 0.0 all-gather.9.cloned.1.call-start
  8.1 0.7 all-gather.9.cloned.1.call-update
  9.4 0.7 pad_maximum_fusion
  10.1 6.1 %all_gather.19 = f32[2,1024]{1,0:T(2,128)S(1)} all-gather(f32[2,256]{1,0:T(2,128)S(1)} %pad_maximum_fusion), channel_id=1, replica_groups=mesh['dom'=8,'feat'=4] {'feat'}, dimensions={1}, use_global_device_ids=true | all-gather | bytes 10240 | tf_op jit(solution)/shard_map/all_gather | solution.py:395
  16.2 1.2 copy-done.3
  17.4 1.1 copy-done.4
  18.5 1.1 copy-done.5
  19.6 0.7 copy-done.6
  20.2 52.3 %project.1 = (bf16[6144,256]{1,0:T(8,128)(2,1)S(1)}, bf16[2048,256]{1,0:T(8,128)(2,1)S(1)}, bf16[512,1024]{1,0:T(8,128)(2,1)S(1)}) custom-call(bf16[2048,256]{1,0:T(8,128)(2,1)S(1)} %copy-done.3, bf16[1024,256]{1,0:T(8,128)(2,1)S(1)} %copy-done.4, bf16[1024,256]{1,0:T(8,128)(2,1)S(1)} %copy-done.5, s32[1,4,4]{2,1,0:T(4,128)S(1)} %copy-done.6), custom_call_target="tpu_custom_call" | custom-call | flops 2147483648 | bytes 104857600 | tf_op jit(solution)/shard_map/project/pallas_call | solution.py:397
  72.6 1.7 %copy-done.7 = bf16[6144,256]{1,0:T(8,128)(2,1)} copy-done((bf16[6144,256]{1,0:T(8,128)(2,1)}, bf16[6144,256]{1,0:T(8,128)(2,1)S(1)}, u32[]{:S(2)}) %copy-start.7) | copy-done | bytes 3145752
  74.2 1.0 copy-done.9
  75.2 0.6 add_multiply_fusion.idx_ref
  75.9 10.9 %edges.1.summed_ref = bf16[2048,256]{1,0:T(8,128)(2,1)} custom-call(s32[96,128]{1,0:T(8,128)} %add_multiply_fusion.idx_ref, s32[1,96]{1,0:T(1,128)} %dst_tile_ref.1, s32[1]{0:T(128)S(6)} %copy.16.count_ref, s32[96,128]{1,0:T(8,128)} %off_ref.1, bf16[6144,256]{1,0:T(8,128)(2,1)} %copy-done.7, bf16[2048,256]{1,0:T(8,128)(2,1)} %copy-done.9), custom_call_target="tpu_custom_call" | custom-call | flops 1610612736 | bytes 104857600 | tf_op jit(solution)/shard_map/edges/pallas_call | solution.py:427
  86.8 0.0 all-gather.5.cloned.1.call-done.we_hbm
  86.8 17.2 %all-gather.9.cloned.1.call-done = bf16[8192,256]{1,0:T(8,128)(2,1)} async-done(((bf16[2048,256]{1,0:T(8,128)(2,1)}), bf16[8192,256]{1,0:T(8,128)(2,1)}) %all-gather.9.cloned.1.call-update) | async-done | bytes 4194320 | tf_op jit(solution)/shard_map/all_gather | solution.py:393
  104.0 2.2 %copy-done = bf16[8192,256]{1,0:T(8,128)(2,1)S(1)} copy-done((bf16[8192,256]{1,0:T(8,128)(2,1)S(1)}, bf16[8192,256]{1,0:T(8,128)(2,1)}, u32[]{:S(2)}) %copy-start) | copy-done | bytes 4194328
  106.2 1.6 %copy-done.1 = bf16[1024,1024]{1,0:T(8,128)(2,1)S(1)} copy-done((bf16[1024,1024]{1,0:T(8,128)(2,1)S(1)}, bf16[1024,1024]{1,0:T(8,128)(2,1)}, u32[]{:S(2)}) %copy-start.1) | copy-done | bytes 2097176
  107.8 1.6 %copy-done.2 = bf16[1024,1024]{1,0:T(8,128)(2,1)S(1)} copy-done((bf16[1024,1024]{1,0:T(8,128)(2,1)S(1)}, bf16[1024,1024]{1,0:T(8,128)(2,1)}, u32[]{:S(2)}) %copy-start.2) | copy-done | bytes 2097176
  109.4 1.2 copy-done.8
  110.6 25.7 %nodes.1 = bf16[2048,256]{1,0:T(8,128)(2,1)S(1)} custom-call(bf16[2048,256]{1,0:T(8,128)(2,1)S(1)} %copy-done.8, bf16[512,1024]{1,0:T(8,128)(2,1)S(1)} %get-tuple-element.10.rows_ref, bf16[1024,1024]{1,0:T(8,128)(2,1)S(1)} %copy-done.1, bf16[4,2048,256]{2,1,0:T(8,128)(2,1)S(1)} %bitcast.3, bf16[1024,1024]{1,0:T(8,128)(2,1)S(1)} %copy-done.2, ...), custom_call_target="tpu_custom_call" | custom-call | flops 4294967296 | bytes 62914560 | tf_op jit(solution)/shard_map/nodes/pallas_call | solution.py:446
  136.3 1.0 copy.17
  (17 shorter events, 0.1 us)
Async XLA Ops:
  6.5 80.3 %all-gather.5.cloned.1.call-start = ((), (), s32[]{:S(2)}) async-start(), calls=%async_computation | async-start | bytes 2621440 | tf_op jit(solution)/shard_map/all_gather | solution.py:392
  7.3 79.6 %all-gather.7.cloned.1.call-start = ((), (), s32[]{:S(2)}) async-start(), calls=%async_computation.1 | async-start | bytes 2621440 | tf_op jit(solution)/shard_map/all_gather | solution.py:394
  8.0 96.0 %all-gather.9.cloned.1.call-start = ((), (), s32[]{:S(2)}) async-start(), calls=%async_computation.2 | async-start | bytes 5242880 | tf_op jit(solution)/shard_map/all_gather | solution.py:393
  16.2 1.2 copy-start.3
  17.4 1.1 copy-start.4
  18.5 1.1 copy-start.5
  19.6 0.7 copy-start.6
  20.2 55.0 %copy-start.10 = (s32[96,128]{1,0:T(8,128)S(1)}, s32[96,128]{1,0:T(8,128)}, u32[]{:S(2)}) copy-start(s32[96,128]{1,0:T(8,128)} %param.24) | copy-start | bytes 147460
  20.2 55.0 %copy-start.11 = (s32[96,128]{1,0:T(8,128)S(1)}, s32[96,128]{1,0:T(8,128)}, u32[]{:S(2)}) copy-start(s32[96,128]{1,0:T(8,128)} %param.22) | copy-start | bytes 147460
  72.6 1.7 %copy-start.7 = (bf16[6144,256]{1,0:T(8,128)(2,1)}, bf16[6144,256]{1,0:T(8,128)(2,1)S(1)}, u32[]{:S(2)}) copy-start(bf16[6144,256]{1,0:T(8,128)(2,1)S(1)} %get-tuple-element.8.table_ref) | copy-start | bytes 9437188
  74.2 1.0 copy-start.9
  104.0 2.2 %copy-start = (bf16[8192,256]{1,0:T(8,128)(2,1)S(1)}, bf16[8192,256]{1,0:T(8,128)(2,1)}, u32[]{:S(2)}) copy-start(bf16[8192,256]{1,0:T(8,128)(2,1)} %all-gather.9.cloned.1.call-done) | copy-start | bytes 12582916
  106.2 1.6 %copy-start.1 = (bf16[1024,1024]{1,0:T(8,128)(2,1)S(1)}, bf16[1024,1024]{1,0:T(8,128)(2,1)}, u32[]{:S(2)}) copy-start(bf16[1024,1024]{1,0:T(8,128)(2,1)} %all-gather.5.cloned.1.call-done.we_hbm) | copy-start | bytes 6291460
  107.8 1.6 %copy-start.2 = (bf16[1024,1024]{1,0:T(8,128)(2,1)S(1)}, bf16[1024,1024]{1,0:T(8,128)(2,1)}, u32[]{:S(2)}) copy-start(bf16[1024,1024]{1,0:T(8,128)(2,1)} %all-gather.7.cloned.1.call-done.wo_hbm) | copy-start | bytes 6291460
  109.4 1.2 copy-start.8
Sparse Core Ops, SparseCore 0:
  8.9 29.6 all-gather.4
  40.1 27.7 all-gather.6
  69.5 34.4 all-gather.8

commit v2 on v1

--- a/solution.py
+++ b/solution.py
@@ -25,12 +25,22 @@
 
 def project_kernel(
     lat_ref,
-    ws_ref,
-    wd_ref,
+    ws_hbm,
+    wd_hbm,
     st_ref,
+    norm_ref,
+    we_own,
+    wi_own,
+    wo_own,
     table_ref,
     recv_ref,
     rows_ref,
+    norm_all,
+    we_all,
+    wi_all,
+    wo_all,
+    ws_ref,
+    wd_ref,
     parts,
     held,
     halo,
@@ -45,6 +55,17 @@
     c_recv,
     h_send,
     h_recv,
+    n_send,
+    n_recv,
+    near_send,
+    near_recv,
+    far_send,
+    far_recv,
+    side_send,
+    side_recv,
+    pass_send,
+    pass_recv,
+    load_sem,
 ):
     nf, nodes, width = parts.shape
     nd = lax.axis_size("dom")
@@ -96,12 +117,76 @@
             )
         )
     own = pltpu.make_async_copy(lat_ref, parts.at[feat], own_sem)
+    loads = [
+        pltpu.make_async_copy(src, dst, load_sem.at[i])
+        for i, (src, dst) in enumerate(
+            (
+                (ws_hbm, ws_ref),
+                (wd_hbm, wd_ref),
+                (we_own, we_all.at[feat]),
+                (wi_own, wi_all.at[feat]),
+                (wo_own, wo_all.at[feat]),
+            )
+        )
+    ]
+
+    def remote(src, dst, send, recv, i, peer):
+        return pltpu.make_async_remote_copy(
+            src_ref=src,
+            dst_ref=dst,
+            send_sem=send.at[i],
+            recv_sem=recv.at[i],
+            device_id=peer,
+            device_id_type=MESH,
+        )
+
+    side = lax.rem(dom, 2)
+    beside = {"dom": dom + 1 - 2 * side}
+
+    def pieces(half):
+        found = []
+        for src, dst, count in ((we_own, we_all, 1), (wo_own, wo_all, 1), (wi_own, wi_all, 2)):
+            size = src.shape[0] // (2 * count)
+            for i in range(count):
+                found.append((src, dst, pl.ds(half * (size * count) + i * size, size)))
+        return found
+
+    mine, other = pieces(side), pieces(1 - side)
+    count = len(mine)
+    weights_near = [
+        remote(src, dst.at[feat], near_send, near_recv, i, {"feat": near})
+        for i, (src, dst) in enumerate(((we_own, we_all), (wi_own, wi_all), (wo_own, wo_all)))
+    ]
+    weights_far = [
+        remote(src.at[at], dst.at[feat, at], far_send, far_recv, i, {"feat": far})
+        for i, (src, dst, at) in enumerate(mine)
+    ]
+    weights_side = [
+        remote(dst.at[far, at], dst.at[far, at], side_send, side_recv, i, beside)
+        for i, (src, dst, at) in enumerate(mine)
+    ]
+    weights_pass = [
+        remote(dst.at[far, at], dst.at[far, at], pass_send, pass_recv, i, {"feat": near})
+        for i, (src, dst, at) in enumerate(mine + other)
+    ]
+    norms = [
+        remote(norm_ref, norm_all.at[feat], n_send, n_recv, 0, {"feat": far}),
+        remote(norm_ref, norm_all.at[feat], n_send, n_recv, 1, {"feat": near}),
+        remote(norm_all.at[far], norm_all.at[far], n_send, n_recv, 2, {"feat": near}),
+    ]
+    norms[0].start()
+    norms[1].start()
+    norm_all[feat] = norm_ref[...]
     for c in range(chunks):
         to_far[c].start()
     own.start()
     for c in range(chunks):
         to_near[c].start()
+    for load in loads:
+        load.start()
     own.wait()
+    loads[0].wait()
+    loads[1].wait()
 
     coarse = []
     for k in range(1, nd):
@@ -134,6 +219,9 @@
     for c in range(chunks):
         to_far[c].wait_recv()
         onward[c].start()
+        if c == chunks - 2:
+            for copy in weights_far:
+                copy.start()
         if c > 0:
             project(c - 1)
     project(chunks - 1)
@@ -167,9 +255,21 @@
         def _(base=base):
             table_ref[pl.ds(base, batch * TILE), :] = jnp.zeros((batch * TILE, width), BF)
 
+    for copy in weights_near:
+        copy.start()
+    norms[0].wait_recv()
+    norms[2].start()
     share = nodes // nf
     for f in range(nf):
         rows_ref[:, f * width : (f + 1) * width] = parts[f, pl.ds(feat * share, share), :]
+
+    for i in range(count):
+        weights_far[i].wait_recv()
+        weights_side[i].start()
+        weights_pass[i].start()
+    for i in range(count):
+        weights_side[i].wait_recv()
+        weights_pass[count + i].start()
 
     for copy, sends, gets in spread:
 
@@ -188,26 +288,51 @@
         to_far[c].wait_send()
         to_near[c].wait_send()
         onward[c].wait_send()
+    for copy in weights_near + weights_pass + norms[1:]:
+        copy.wait_send()
+        copy.wait_recv()
+    for copy in weights_far + weights_side + norms[:1]:
+        copy.wait_send()
+    for load in loads[2:]:
+        load.wait()
 
 
 UNROLL = 4
 
 
 def edge_kernel(
-    idx_ref, dst_tile_ref, count_ref, off_ref, table_ref, recv_ref, out_ref, wide, acc, *slots
+    idx_ref,
+    dst_tile_ref,
+    count_ref,
+    off_ref,
+    table_hbm,
+    recv_hbm,
+    out_ref,
+    table_ref,
+    recv_ref,
+    wide,
+    acc,
+    sems,
+    *slots,
 ):
     rows, width = table_ref.shape
     half = width // 2
     block = 8 * TILE
 
-    @pl.loop(0, rows // block)
-    def _(i):
-        part = table_ref[pl.ds(pl.multiple_of(i * block, block), block), :].astype(F32)
-        at = pl.multiple_of(i * (2 * block), 2 * block)
-        wide[pl.ds(at, block, stride=2), :] = part[:, :half]
-        wide[pl.ds(at + 1, block, stride=2), :] = part[:, half:]
-
+    loads = []
+    for i in range(rows // block):
+        at = pl.ds(i * block, block)
+        loads.append(pltpu.make_async_copy(table_hbm.at[at], table_ref.at[at], sems.at[i]))
+    loads.append(pltpu.make_async_copy(recv_hbm, recv_ref, sems.at[rows // block]))
+    for load in loads:
+        load.start()
     acc[...] = jnp.zeros_like(acc)
+    for i in range(rows // block):
+        loads[i].wait()
+        part = table_ref[pl.ds(i * block, block), :].astype(F32)
+        wide[pl.ds(2 * i * block, block, stride=2), :] = part[:, :half]
+        wide[pl.ds(2 * i * block + 1, block, stride=2), :] = part[:, half:]
+    loads[-1].wait()
     ids = lax.broadcasted_iota(jnp.int32, (TILE, TILE), 0)
     count = count_ref[0]
 
@@ -238,13 +363,13 @@
 
 def node_kernel(
     summed_ref,
-    rows_ref,
+    rows_hbm,
     we_hbm,
     wi_hbm,
     wo_hbm,
-    gain_ref,
-    bias_ref,
+    norm_ref,
     out_ref,
+    rows_ref,
     we,
     wi,
     wo,
@@ -270,7 +395,15 @@
         )
     loads = [
         pltpu.make_async_copy(src, dst, load_sem.at[i])
-        for i, (src, dst) in enumerate(((wi_hbm, wi), (we_hbm, we), (wo_hbm, wo)))
+        for i, (src, dst) in enumerate(
+            (
+                (rows_hbm, rows_ref),
+                (wi_hbm, wi),
+                (summed_ref.at[pl.ds(feat * share, share)], taken.at[feat]),
+                (we_hbm, we),
+                (wo_hbm, wo),
+            )
+        )
     ]
     pl.semaphore_wait(barrier, nf - 1)
 
@@ -289,9 +422,10 @@
             ins[c, k].start()
     for load in loads:
         load.start()
-    taken[feat] = summed_ref[pl.ds(feat * share, share), :]
-    for load in loads:
-        load.wait()
+    gain = jnp.concatenate([norm_ref[f, 0:1, :] for f in range(nf)], axis=1)
+    bias = jnp.concatenate([norm_ref[f, 1:2, :] for f in range(nf)], axis=1)
+    loads[0].wait()
+    loads[1].wait()
 
     outs = []
     keeps = []
@@ -303,10 +437,13 @@
         ]
         for k in (2, 1, 3):
             ins[c, k].wait_recv()
+        if c == 0:
+            for load in loads[2:]:
+                load.wait()
         total = jnp.zeros((step, full), F32)
         for f in range(nf):
             term = jnp.dot(
-                taken[f, rows, :], we[f * width : (f + 1) * width, :], preferred_element_type=F32
+                taken[f, rows, :], we[f], preferred_element_type=F32
             )
             total = total + term.astype(BF).astype(F32)
         aggregate = total.astype(BF)
@@ -314,11 +451,11 @@
         for f in range(nf):
             pre = first[f] + jnp.dot(aggregate, wi[f, full:, :], preferred_element_type=F32)
             hidden = swish(pre).astype(BF)
-            term = jnp.dot(hidden, wo[f * width : (f + 1) * width, :], preferred_element_type=F32)
+            term = jnp.dot(hidden, wo[f], preferred_element_type=F32)
             update = update + term.astype(BF).astype(F32)
         average = jnp.sum(update, axis=1, keepdims=True) / full
         spread = jnp.sum(update * update, axis=1, keepdims=True) / full - average * average
-        normed = (update - average) * lax.rsqrt(spread + epsilon) * gain_ref[...] + bias_ref[...]
+        normed = (update - average) * lax.rsqrt(spread + epsilon) * gain + bias
         result = (lat.astype(F32) + normed).astype(BF)
         for f in range(nf):
             given[f, rows, :] = result[:, f * width : (f + 1) * width]
@@ -389,21 +526,24 @@
     edge_tiles = src_tile.shape[0]
     chunks = 8
 
-    we = lax.all_gather(w_edge_out, "feat", axis=0, tiled=True)
-    wi = lax.all_gather(w_node_in, "feat", axis=0)
-    wo = lax.all_gather(w_node_out, "feat", axis=0, tiled=True)
-    norm = lax.all_gather(jnp.stack([norm_gain, norm_bias]), "feat", axis=1, tiled=True)
-
-    table, received, rows = pl.pallas_call(
+    norm = jnp.stack([norm_gain, norm_bias])
+
+    table, received, rows, norms, we, wi, wo = pl.pallas_call(
         project_kernel,
         out_shape=(
             jax.ShapeDtypeStruct((table_rows, width), BF),
             jax.ShapeDtypeStruct((nodes, width), BF),
             jax.ShapeDtypeStruct((share, full), BF),
+            jax.ShapeDtypeStruct((nf, 2, width), F32),
+            jax.ShapeDtypeStruct((nf, width, full), BF),
+            jax.ShapeDtypeStruct((nf, 2 * full, width), BF),
+            jax.ShapeDtypeStruct((nf, width, full), BF),
         ),
-        in_specs=[hbm(), vmem(), vmem(), smem()],
-        out_specs=(vmem(), vmem(), vmem()),
+        in_specs=[hbm(), hbm(), hbm(), smem(), vmem(), hbm(), hbm(), hbm()],
+        out_specs=(vmem(), vmem(), vmem(), vmem(), hbm(), hbm(), hbm()),
         scratch_shapes=[
+            pltpu.VMEM((full, width), BF),
+            pltpu.VMEM((full, width), BF),
             pltpu.VMEM((nf, nodes, width), BF),
             pltpu.VMEM((nodes // TILE, TILE, width), BF),
             pltpu.VMEM((rounds, batch * TILE, width), BF),
@@ -413,6 +553,17 @@
             dma(nd),
             dma(rounds),
             dma(rounds),
+            dma(3),
+            dma(3),
+            dma(3),
+            dma(3),
+            dma(4),
+            dma(4),
+            dma(4),
+            dma(4),
+            dma(8),
+            dma(8),
+            dma(5),
         ],
         compiler_params=pltpu.CompilerParams(
             collective_id=0, has_side_effects=True, vmem_limit_bytes=40 * MIB
@@ -421,17 +572,20 @@
             flops=4 * nodes * full * width, bytes_accessed=100 * MIB, transcendentals=0
         ),
         name="project",
-    )(latents, w_src, w_dst, send_tiles)
+    )(latents, w_src, w_dst, send_tiles, norm, w_edge_out, w_node_in, w_node_out)
 
     index = (src_tile * TILE + src_off) * 2
     summed = pl.pallas_call(
         edge_kernel,
         out_shape=jax.ShapeDtypeStruct((nodes, width), BF),
-        in_specs=[smem(), smem(), smem(), vmem(), vmem(), vmem()],
+        in_specs=[smem(), smem(), smem(), vmem(), hbm(), hbm()],
         out_specs=vmem(),
         scratch_shapes=[
+            pltpu.VMEM((table_rows, width), BF),
+            pltpu.VMEM((nodes, width), BF),
             pltpu.VMEM((2 * table_rows, width // 2), F32),
             pltpu.VMEM((nodes, width), F32),
+            dma(table_rows // (8 * TILE) + 1),
             *[pltpu.VMEM((2 * TILE, width // 2), F32) for _ in range(UNROLL)],
         ],
         compiler_params=pltpu.CompilerParams(vmem_limit_bytes=56 * MIB),
@@ -446,15 +600,16 @@
     return pl.pallas_call(
         node_kernel,
         out_shape=jax.ShapeDtypeStruct((nodes, width), BF),
-        in_specs=[vmem(), vmem(), hbm(), hbm(), hbm(), vmem(), vmem()],
+        in_specs=[hbm(), hbm(), hbm(), hbm(), hbm(), vmem()],
         out_specs=hbm(),
         scratch_shapes=[
-            pltpu.VMEM((full, full), BF),
+            pltpu.VMEM((share, full), BF),
+            pltpu.VMEM((nf, width, full), BF),
             pltpu.VMEM((nf, 2 * full, width), BF),
-            pltpu.VMEM((full, full), BF),
+            pltpu.VMEM((nf, width, full), BF),
             pltpu.VMEM((nf, share, width), BF),
             pltpu.VMEM((nf, share, width), BF),
-            dma(3),
+            dma(5),
             dma(4),
             dma(4, nf),
             dma(4, nf),
@@ -468,7 +623,7 @@
             flops=8 * share * full * full, bytes_accessed=60 * MIB, transcendentals=share * full
         ),
         name="nodes",
-    )(summed, rows, we, wi, wo, norm[0:1], norm[1:2])
+    )(summed, rows, we, wi, wo, norms)
 
 
 def solution(mesh):

time: 144 us -> 140 us (0.972)
  the two profiles are of different devices: /device:TPU:0 before, /device:TPU:13 now
where the time goes in v2:
time: 140 us; the launch traced here: 138 us
  Pallas kernels  120 us (86%)
  local copies, waits for them, and re-layouts  15.1 us (11%)
  other arithmetic  2.15 us (2%)
    pallas_call x1, Pallas kernels, body(): pl.pallas_call(project_kernel, out_shape=(jax.ShapeDtypeStruct((table_row...  72.3 us
    pallas_call x1, Pallas kernels, body(): pl.pallas_call(node_kernel, out_shape=jax.ShapeDtypeStruct((nodes, width)...  25.6 us
    pallas_call x1, Pallas kernels, body(): pl.pallas_call(edge_kernel, out_shape=jax.ShapeDtypeStruct((nodes, width)...  21.9 us
    unnamed x27, local copies, waits for them, and re-layouts  15.1 us

profile of v2, /device:TPU:13, one launch (start us, length us, event | category | flops | bytes accessed | tf_op | source)
XLA Modules:
  0.0 137.8 jit_solution(7958397592936627785)
XLA Ops:
  0.7 0.7 pad_maximum_fusion.norm_ref
  1.4 1.4 %add_multiply_fusion.idx_ref = s32[96,128]{1,0:T(8,128)} fusion(s32[96,128]{1,0:T(8,128)} %param.24, s32[96,128]{1,0:T(8,128)} %param.22), kind=kLoop, calls=%fused_computation | loop fusion | flops 36864 | bytes 147456 | tf_op jit(solution)/shard_map/mul | solution.py:577
  2.8 0.0 copy-start
  2.8 1.2 copy-done
  4.0 0.0 copy-start.1
  4.0 1.2 copy-done.1
  5.3 0.0 copy-start.2
  5.3 1.0 copy-done.2
  6.3 1.0 copy-done.3
  7.3 1.0 copy-done.4
  8.4 1.0 copy-done.5
  9.4 0.7 copy-done.6
  10.1 72.3 %project.1 = (bf16[6144,256]{1,0:T(8,128)(2,1)S(1)}, bf16[2048,256]{1,0:T(8,128)(2,1)S(1)}, bf16[512,1024]{1,0:T(8,128)(2,1)S(1)}, f32[4,2,256]{2,1,0:T(2,128)S(...) custom-call(bf16[2048,256]{1,0:T(8,128)(2,1)S(1)} %copy-done, ...), custom_call_target="tpu_custom_call" | custom-call | flops 2147483648 | bytes 104857600 | tf_op jit(solution)/shard_map/project/pallas_call | solution.py:531
  82.4 0.0 copy-start.7
  82.4 1.7 %copy-done.7 = bf16[6144,256]{1,0:T(8,128)(2,1)} copy-done((bf16[6144,256]{1,0:T(8,128)(2,1)}, bf16[6144,256]{1,0:T(8,128)(2,1)S(1)}, u32[]{:S(2)}) %copy-start.7) | copy-done | bytes 3145752
  84.1 1.0 copy-done.8
  85.1 1.4 %copy-done.11 = bf16[4,256,1024]{2,1,0:T(8,128)(2,1)} copy-done((bf16[4,256,1024]{2,1,0:T(8,128)(2,1)}, bf16[4,256,1024]{2,1,0:T(8,128)(2,1)S(1)}, u32[]{:S(2)}) %copy-start.11) | copy-done | bytes 2097176
  86.5 21.9 %edges.1.summed_ref = bf16[2048,256]{1,0:T(8,128)(2,1)} custom-call(s32[96,128]{1,0:T(8,128)} %add_multiply_fusion.idx_ref, s32[1,96]{1,0:T(1,128)} %dst_tile_ref.1, s32[1]{0:T(128)S(6)} %copy.16.count_ref, s32[96,128]{1,0:T(8,128)} %off_ref.1, bf16[6144,256]{1,0:T(8,128)(2,1)} %copy-done.7, bf16[2048,256]{1,0:T(8,128)(2,1)} %copy-done.8), custom_call_target="tpu_custom_call" | custom-call | flops 1610612736 | bytes 104857600 | tf_op jit(solution)/shard_map/edges/pallas_call | solution.py:578
  108.4 0.0 copy-done.10
  108.4 0.0 copy-start.9
  108.4 1.2 copy-done.9
  109.6 1.6 %copy-done.12 = bf16[4,256,1024]{2,1,0:T(8,128)(2,1)S(1)} copy-done((bf16[4,256,1024]{2,1,0:T(8,128)(2,1)S(1)}, bf16[4,256,1024]{2,1,0:T(8,128)(2,1)}, u32[]{:S(2)}) %copy-start.12) | copy-done | bytes 2097176
  111.2 25.6 %nodes.1 = bf16[2048,256]{1,0:T(8,128)(2,1)S(1)} custom-call(bf16[2048,256]{1,0:T(8,128)(2,1)S(1)} %copy-done.9, bf16[512,1024]{1,0:T(8,128)(2,1)S(1)} %get-tuple-element.14.rows_hbm, bf16[4,256,1024]{2,1,0:T(8,128)(2,1)S(1)} %get-tuple-element.15.we_hbm, bf16[4,2048,256]{2,1,0:T(8,128)(2,1)S(1)} %copy-done.10, bf16[4,256,1024]{2,1,0:T(8,128)(2,1)S(1)} %copy-done.12, ...), custom_call_target="tpu_custom_call" | custom-call | flops 4294967296 | bytes 62914560 | tf_op jit(solution)/shard_map/nodes/pallas_call | solution.py:600
  136.8 1.0 copy.17
  (8 shorter events, 0.0 us)
Async XLA Ops:
  2.8 1.2 copy-start
  4.0 1.2 copy-start.1
  5.3 1.0 copy-start.2
  6.3 1.0 copy-start.3
  7.3 1.0 copy-start.4
  8.4 1.0 copy-start.5
  9.4 0.7 copy-start.6
  82.4 1.7 %copy-start.7 = (bf16[6144,256]{1,0:T(8,128)(2,1)}, bf16[6144,256]{1,0:T(8,128)(2,1)S(1)}, u32[]{:S(2)}) copy-start(bf16[6144,256]{1,0:T(8,128)(2,1)S(1)} %get-tuple-element.12.table_hbm) | copy-start | bytes 9437188
  84.1 1.0 copy-start.8
  85.1 1.4 %copy-start.11 = (bf16[4,256,1024]{2,1,0:T(8,128)(2,1)}, bf16[4,256,1024]{2,1,0:T(8,128)(2,1)S(1)}, u32[]{:S(2)}) copy-start(bf16[4,256,1024]{2,1,0:T(8,128)(2,1)S(1)} %get-tuple-element.17.wo_hbm) | copy-start | bytes 6291460
  86.5 21.9 %copy-start.10 = (bf16[4,2048,256]{2,1,0:T(8,128)(2,1)S(1)}, bf16[4,2048,256]{2,1,0:T(8,128)(2,1)}, u32[]{:S(2)}) copy-start(bf16[4,2048,256]{2,1,0:T(8,128)(2,1)} %get-tuple-element.16.wi_hbm) | copy-start | bytes 12582916
  108.4 1.2 copy-start.9
  109.6 1.6 %copy-start.12 = (bf16[4,256,1024]{2,1,0:T(8,128)(2,1)S(1)}, bf16[4,256,1024]{2,1,0:T(8,128)(2,1)}, u32[]{:S(2)}) copy-start(bf16[4,256,1024]{2,1,0:T(8,128)(2,1)} %copy-done.11) | copy-start | bytes 6291460

commit v3 on v2

--- a/solution.py
+++ b/solution.py
@@ -61,8 +61,6 @@
     near_recv,
     far_send,
     far_recv,
-    side_send,
-    side_recv,
     pass_send,
     pass_recv,
     load_sem,
@@ -140,34 +138,22 @@
             device_id_type=MESH,
         )
 
-    side = lax.rem(dom, 2)
-    beside = {"dom": dom + 1 - 2 * side}
-
-    def pieces(half):
-        found = []
-        for src, dst, count in ((we_own, we_all, 1), (wo_own, wo_all, 1), (wi_own, wi_all, 2)):
-            size = src.shape[0] // (2 * count)
-            for i in range(count):
-                found.append((src, dst, pl.ds(half * (size * count) + i * size, size)))
-        return found
-
-    mine, other = pieces(side), pieces(1 - side)
-    count = len(mine)
+    pieces = []
+    for src, dst in ((we_own, we_all), (wo_own, wo_all)):
+        size = width // 2
+        for i in range(2):
+            pieces.append((src, dst, pl.ds(i * size, size)))
     weights_near = [
         remote(src, dst.at[feat], near_send, near_recv, i, {"feat": near})
         for i, (src, dst) in enumerate(((we_own, we_all), (wi_own, wi_all), (wo_own, wo_all)))
     ]
     weights_far = [
         remote(src.at[at], dst.at[feat, at], far_send, far_recv, i, {"feat": far})
-        for i, (src, dst, at) in enumerate(mine)
-    ]
-    weights_side = [
-        remote(dst.at[far, at], dst.at[far, at], side_send, side_recv, i, beside)
-        for i, (src, dst, at) in enumerate(mine)
+        for i, (src, dst, at) in enumerate(pieces)
     ]
     weights_pass = [
         remote(dst.at[far, at], dst.at[far, at], pass_send, pass_recv, i, {"feat": near})
-        for i, (src, dst, at) in enumerate(mine + other)
+        for i, (src, dst, at) in enumerate(pieces)
     ]
     norms = [
         remote(norm_ref, norm_all.at[feat], n_send, n_recv, 0, {"feat": far}),
@@ -263,13 +249,9 @@
     for f in range(nf):
         rows_ref[:, f * width : (f + 1) * width] = parts[f, pl.ds(feat * share, share), :]
 
-    for i in range(count):
-        weights_far[i].wait_recv()
-        weights_side[i].start()
-        weights_pass[i].start()
-    for i in range(count):
-        weights_side[i].wait_recv()
-        weights_pass[count + i].start()
+    for came, passed in zip(weights_far, weights_pass):
+        came.wait_recv()
+        passed.start()
 
     for copy, sends, gets in spread:
 
@@ -291,7 +273,7 @@
     for copy in weights_near + weights_pass + norms[1:]:
         copy.wait_send()
         copy.wait_recv()
-    for copy in weights_far + weights_side + norms[:1]:
+    for copy in weights_far + norms[:1]:
         copy.wait_send()
     for load in loads[2:]:
         load.wait()
@@ -366,6 +348,7 @@
     rows_hbm,
     we_hbm,
     wi_hbm,
+    wi_far,
     wo_hbm,
     norm_ref,
     out_ref,
@@ -381,6 +364,8 @@
     in_recv,
     out_send,
     out_recv,
+    pass_send,
+    pass_recv,
 ):
     nf, share, width = taken.shape
     full = nf * width
@@ -393,12 +378,25 @@
         pl.semaphore_signal(
             barrier, inc=1, device_id={"feat": lax.rem(feat + k, nf)}, device_id_type=MESH
         )
+    x, core = feat // 2, feat % 2
+    near = x * 2 + (1 - core)
+    far = (1 - x) * 2 + core
+    passed = pltpu.make_async_remote_copy(
+        src_ref=wi_far,
+        dst_ref=wi.at[far],
+        send_sem=pass_send.at[0],
+        recv_sem=pass_recv.at[0],
+        device_id={"feat": near},
+        device_id_type=MESH,
+    )
     loads = [
         pltpu.make_async_copy(src, dst, load_sem.at[i])
         for i, (src, dst) in enumerate(
             (
                 (rows_hbm, rows_ref),
-                (wi_hbm, wi),
+                (wi_hbm.at[feat], wi.at[feat]),
+                (wi_hbm.at[near], wi.at[near]),
+                (wi_far, wi.at[far]),
                 (summed_ref.at[pl.ds(feat * share, share)], taken.at[feat]),
                 (we_hbm, we),
                 (wo_hbm, wo),
@@ -422,10 +420,12 @@
             ins[c, k].start()
     for load in loads:
         load.start()
+    passed.start()
     gain = jnp.concatenate([norm_ref[f, 0:1, :] for f in range(nf)], axis=1)
     bias = jnp.concatenate([norm_ref[f, 1:2, :] for f in range(nf)], axis=1)
-    loads[0].wait()
-    loads[1].wait()
+    for load in loads[:4]:
+        load.wait()
+    passed.wait_recv()
 
     outs = []
     keeps = []
@@ -438,7 +438,7 @@
         for k in (2, 1, 3):
             ins[c, k].wait_recv()
         if c == 0:
-            for load in loads[2:]:
+            for load in loads[4:]:
                 load.wait()
         total = jnp.zeros((step, full), F32)
         for f in range(nf):
@@ -475,6 +475,7 @@
         keep = pltpu.make_async_copy(given.at[feat, rows], out_ref.at[place], keep_sem.at[c])
         keep.start()
         keeps.append(keep)
+    passed.wait_send()
     for keep in keeps:
         keep.wait()
     for copy in outs:
@@ -561,18 +562,19 @@
             dma(4),
             dma(4),
             dma(4),
-            dma(8),
-            dma(8),
             dma(5),
         ],
         compiler_params=pltpu.CompilerParams(
-            collective_id=0, has_side_effects=True, vmem_limit_bytes=40 * MIB
+            collective_id=0, has_side_effects=True, vmem_limit_bytes=62 * MIB
         ),
         cost_estimate=pl.CostEstimate(
             flops=4 * nodes * full * width, bytes_accessed=100 * MIB, transcendentals=0
         ),
         name="project",
     )(latents, w_src, w_dst, send_tiles, norm, w_edge_out, w_node_in, w_node_out)
+
+    crossing, norms = lax.optimization_barrier((w_node_in, norms))
+    wi_far = lax.ppermute(crossing, "feat", [(0, 2), (2, 0), (1, 3), (3, 1)])
 
     index = (src_tile * TILE + src_off) * 2
     summed = pl.pallas_call(
@@ -588,7 +590,7 @@
             dma(table_rows // (8 * TILE) + 1),
             *[pltpu.VMEM((2 * TILE, width // 2), F32) for _ in range(UNROLL)],
         ],
-        compiler_params=pltpu.CompilerParams(vmem_limit_bytes=56 * MIB),
+        compiler_params=pltpu.CompilerParams(vmem_limit_bytes=62 * MIB),
         cost_estimate=pl.CostEstimate(
             flops=4 * edge_tiles * TILE * TILE * width,
             bytes_accessed=100 * MIB,
@@ -600,7 +602,7 @@
     return pl.pallas_call(
         node_kernel,
         out_shape=jax.ShapeDtypeStruct((nodes, width), BF),
-        in_specs=[hbm(), hbm(), hbm(), hbm(), hbm(), vmem()],
+        in_specs=[hbm(), hbm(), hbm(), hbm(), hbm(), hbm(), vmem()],
         out_specs=hbm(),
         scratch_shapes=[
             pltpu.VMEM((share, full), BF),
@@ -609,21 +611,23 @@
             pltpu.VMEM((nf, width, full), BF),
             pltpu.VMEM((nf, share, width), BF),
             pltpu.VMEM((nf, share, width), BF),
-            dma(5),
+            dma(7),
             dma(4),
             dma(4, nf),
             dma(4, nf),
             dma(4, nf),
             dma(4, nf),
+            dma(1),
+            dma(1),
         ],
         compiler_params=pltpu.CompilerParams(
-            collective_id=1, has_side_effects=True, vmem_limit_bytes=40 * MIB
+            collective_id=1, has_side_effects=True, vmem_limit_bytes=62 * MIB
         ),
         cost_estimate=pl.CostEstimate(
             flops=8 * share * full * full, bytes_accessed=60 * MIB, transcendentals=share * full
         ),
         name="nodes",
-    )(summed, rows, we, wi, wo, norms)
+    )(summed, rows, we, wi, wi_far, wo, norms)
 
 
 def solution(mesh):

time: 140 us -> 130 us (0.929)
  the two profiles are of different devices: /device:TPU:13 before, /device:TPU:0 now
where the time goes in v3:
time: 130 us
  Pallas kernels  114 us (88%)
  waiting for transfers between devices  9.76 us (8%)
  local copies, waits for them, and re-layouts  2.27 us (2%)
  other arithmetic  1.9 us (1%)
  starting transfers between devices  1.56 us (1%)
    pallas_call x1, Pallas kernels, body(): pl.pallas_call(project_kernel, out_shape=(jax.ShapeDtypeStruct((table_row...  74.8 us
    pallas_call x1, Pallas kernels, body(): pl.pallas_call(node_kernel, out_shape=jax.ShapeDtypeStruct((nodes, width)...  26.7 us
    pallas_call x1, Pallas kernels, body(): pl.pallas_call(edge_kernel, out_shape=jax.ShapeDtypeStruct((nodes, width)...  12.2 us
    ppermute x1, waiting for transfers between devices, body(): wi_far = lax.ppermute(crossing, 'feat', [(0, 2), (2, 0), (1, 3), (3, 1)])  9.76 us
  transfers between devices with their start and end apart: 1, of which 1 were waited for; matrix products, arithmetic and copies ran while one was open for 0% of the time, Pallas kernels for 9%

profile of v3, /device:TPU:0, one launch (start us, length us, event | category | flops | bytes accessed | tf_op | source)
XLA Modules:
  0.0 129.9 jit_solution(6913158104948093191)
XLA Ops:
  0.0 1.3 pad_maximum_fusion.norm_ref
  1.3 0.0 copy-start.2
  1.3 0.0 copy-start
  1.3 0.0 copy-start.1
  1.3 74.8 %project.1 = (bf16[6144,256]{1,0:T(8,128)(2,1)}, bf16[2048,256]{1,0:T(8,128)(2,1)}, bf16[512,1024]{1,0:T(8,128)(2,1)}, f32[4,2,256]{2,1,0:T(2,128)}, bf16[4,256,...) custom-call(bf16[2048,256]{1,0:T(8,128)(2,1)} %lat_ref.1, ...), custom_call_target="tpu_custom_call" | custom-call | flops 2147483648 | bytes 104857600 | tf_op jit(solution)/shard_map/project/pallas_call | solution.py:532
  76.1 0.0 copy-done.2
  76.1 1.6 %collective-permute-start = (bf16[2048,256]{1,0:T(8,128)(2,1)S(1)}, bf16[2048,256]{1,0:T(8,128)(2,1)}, u32[]{:S(2)}, u32[]{:S(2)}) collective-permute-start(bf16[2048,256]{1,0:T(8,128)(2,1)S(1)} %copy-done.2), channel_id=1, source_target_pairs={{0,2},{2,0},{1,3},{3,1},{4,6},{6,4},{5,7},{7,5},{8,10},{10,8},{9,1... | collective-permute-start | bytes 3145736 | tf_op jit(solution)/shard_map/ppermute | solution.py:577
  78.3 0.0 copy-done
  78.3 0.0 copy-done.1
  78.3 0.6 add_multiply_fusion.idx_ref
  78.9 12.2 %edges.1.summed_ref = bf16[2048,256]{1,0:T(8,128)(2,1)} custom-call(s32[96,128]{1,0:T(8,128)} %add_multiply_fusion.idx_ref, s32[1,96]{1,0:T(1,128)} %dst_tile_ref.1, s32[1]{0:T(128)S(6)} %copy.16.count_ref, s32[96,128]{1,0:T(8,128)} %off_ref.1, bf16[6144,256]{1,0:T(8,128)(2,1)} %get-tuple-element.14.table_hbm, bf16[2048,256]{1,0:T(8,128)(2,1)} %get-tuple-element.15.recv_hbm), custom_call_target="tpu_custom_call" | custom-call | flops 1610612736 | bytes 104857600 | tf_op jit(solution)/shard_map/edges/pallas_call | solution.py:580
  91.1 9.8 %collective-permute-done.wi_far = bf16[2048,256]{1,0:T(8,128)(2,1)} collective-permute-done((bf16[2048,256]{1,0:T(8,128)(2,1)S(1)}, bf16[2048,256]{1,0:T(8,128)(2,1)}, u32[]{:S(2)}, u32[]{:S(2)}) %collective-permute-start) | collective-permute-done | bytes 1048608 | tf_op jit(solution)/shard_map/ppermute | solution.py:577
  100.9 26.7 %nodes.1 = bf16[2048,256]{1,0:T(8,128)(2,1)} custom-call(bf16[2048,256]{1,0:T(8,128)(2,1)} %edges.1.summed_ref, bf16[512,1024]{1,0:T(8,128)(2,1)} %get-tuple-element.16.rows_hbm, bf16[4,256,1024]{2,1,0:T(8,128)(2,1)} %get-tuple-element.17.we_hbm, bf16[4,2048,256]{2,1,0:T(8,128)(2,1)} %get-tuple-element.18.wi_hbm, ...), custom_call_target="tpu_custom_call" | custom-call | flops 4294967296 | bytes 62914560 | tf_op jit(solution)/shard_map/nodes/pallas_call | solution.py:602
  127.6 2.3 %copy.17 = bf16[2048,256]{1,0:T(8,128)(2,1)} copy(bf16[2048,256]{1,0:T(8,128)(2,1)} %nodes.1) | data formatting | bytes 2097152
Async XLA Ops:
  1.3 74.8 %copy-start.2 = (bf16[2048,256]{1,0:T(8,128)(2,1)S(1)}, bf16[2048,256]{1,0:T(8,128)(2,1)}, u32[]{:S(2)}) copy-start(bf16[2048,256]{1,0:T(8,128)(2,1)} %wi_own.1) | copy-start | bytes 3145732
  1.3 77.0 %copy-start = (s32[96,128]{1,0:T(8,128)S(1)}, s32[96,128]{1,0:T(8,128)}, u32[]{:S(2)}) copy-start(s32[96,128]{1,0:T(8,128)} %param.24) | copy-start | bytes 147460
  1.3 77.0 %copy-start.1 = (s32[96,128]{1,0:T(8,128)S(1)}, s32[96,128]{1,0:T(8,128)}, u32[]{:S(2)}) copy-start(s32[96,128]{1,0:T(8,128)} %param.22) | copy-start | bytes 147460
  76.1 24.8 %collective-permute-start = (bf16[2048,256]{1,0:T(8,128)(2,1)S(1)}, bf16[2048,256]{1,0:T(8,128)(2,1)}, u32[]{:S(2)}, u32[]{:S(2)}) collective-permute-start(bf16[2048,256]{1,0:T(8,128)(2,1)S(1)} %copy-done.2), channel_id=1, source_target_pairs={{0,2},{2,0},{1,3},{3,1},{4,6},{6,4},{5,7},{7,5},{8,10},{10,8},{9,1... | collective-permute-start | bytes 3145736 | tf_op jit(solution)/shard_map/ppermute | solution.py:577

commit v4 on v3

--- a/solution.py
+++ b/solution.py
@@ -29,16 +29,12 @@
     wd_hbm,
     st_ref,
     norm_ref,
-    we_own,
     wi_own,
-    wo_own,
     table_ref,
     recv_ref,
     rows_ref,
     norm_all,
-    we_all,
     wi_all,
-    wo_all,
     ws_ref,
     wd_ref,
     parts,
@@ -59,10 +55,6 @@
     n_recv,
     near_send,
     near_recv,
-    far_send,
-    far_recv,
-    pass_send,
-    pass_recv,
     load_sem,
 ):
     nf, nodes, width = parts.shape
@@ -121,9 +113,7 @@
             (
                 (ws_hbm, ws_ref),
                 (wd_hbm, wd_ref),
-                (we_own, we_all.at[feat]),
                 (wi_own, wi_all.at[feat]),
-                (wo_own, wo_all.at[feat]),
             )
         )
     ]
@@ -138,23 +128,7 @@
             device_id_type=MESH,
         )
 
-    pieces = []
-    for src, dst in ((we_own, we_all), (wo_own, wo_all)):
-        size = width // 2
-        for i in range(2):
-            pieces.append((src, dst, pl.ds(i * size, size)))
-    weights_near = [
-        remote(src, dst.at[feat], near_send, near_recv, i, {"feat": near})
-        for i, (src, dst) in enumerate(((we_own, we_all), (wi_own, wi_all), (wo_own, wo_all)))
-    ]
-    weights_far = [
-        remote(src.at[at], dst.at[feat, at], far_send, far_recv, i, {"feat": far})
-        for i, (src, dst, at) in enumerate(pieces)
-    ]
-    weights_pass = [
-        remote(dst.at[far, at], dst.at[far, at], pass_send, pass_recv, i, {"feat": near})
-        for i, (src, dst, at) in enumerate(pieces)
-    ]
+    weights_near = remote(wi_own, wi_all.at[feat], near_send, near_recv, 0, {"feat": near})
     norms = [
         remote(norm_ref, norm_all.at[feat], n_send, n_recv, 0, {"feat": far}),
         remote(norm_ref, norm_all.at[feat], n_send, n_recv, 1, {"feat": near}),
@@ -205,9 +179,6 @@
     for c in range(chunks):
         to_far[c].wait_recv()
         onward[c].start()
-        if c == chunks - 2:
-            for copy in weights_far:
-                copy.start()
         if c > 0:
             project(c - 1)
     project(chunks - 1)
@@ -241,17 +212,12 @@
         def _(base=base):
             table_ref[pl.ds(base, batch * TILE), :] = jnp.zeros((batch * TILE, width), BF)
 
-    for copy in weights_near:
-        copy.start()
+    weights_near.start()
     norms[0].wait_recv()
     norms[2].start()
     share = nodes // nf
     for f in range(nf):
         rows_ref[:, f * width : (f + 1) * width] = parts[f, pl.ds(feat * share, share), :]
-
-    for came, passed in zip(weights_far, weights_pass):
-        came.wait_recv()
-        passed.start()
 
     for copy, sends, gets in spread:
 
@@ -270,11 +236,10 @@
         to_far[c].wait_send()
         to_near[c].wait_send()
         onward[c].wait_send()
-    for copy in weights_near + weights_pass + norms[1:]:
+    for copy in [weights_near] + norms[1:]:
         copy.wait_send()
         copy.wait_recv()
-    for copy in weights_far + norms[:1]:
-        copy.wait_send()
+    norms[0].wait_send()
     for load in loads[2:]:
         load.wait()
 
@@ -527,21 +492,21 @@
     edge_tiles = src_tile.shape[0]
     chunks = 8
 
+    we = lax.all_gather(w_edge_out, "feat", axis=0)
+    wo = lax.all_gather(w_node_out, "feat", axis=0)
     norm = jnp.stack([norm_gain, norm_bias])
 
-    table, received, rows, norms, we, wi, wo = pl.pallas_call(
+    table, received, rows, norms, wi = pl.pallas_call(
         project_kernel,
         out_shape=(
             jax.ShapeDtypeStruct((table_rows, width), BF),
             jax.ShapeDtypeStruct((nodes, width), BF),
             jax.ShapeDtypeStruct((share, full), BF),
             jax.ShapeDtypeStruct((nf, 2, width), F32),
-            jax.ShapeDtypeStruct((nf, width, full), BF),
             jax.ShapeDtypeStruct((nf, 2 * full, width), BF),
-            jax.ShapeDtypeStruct((nf, width, full), BF),
         ),
-        in_specs=[hbm(), hbm(), hbm(), smem(), vmem(), hbm(), hbm(), hbm()],
-        out_specs=(vmem(), vmem(), vmem(), vmem(), hbm(), hbm(), hbm()),
+        in_specs=[hbm(), hbm(), hbm(), smem(), vmem(), hbm()],
+        out_specs=(vmem(), vmem(), vmem(), vmem(), hbm()),
         scratch_shapes=[
             pltpu.VMEM((full, width), BF),
             pltpu.VMEM((full, width), BF),
@@ -556,13 +521,9 @@
             dma(rounds),
             dma(3),
             dma(3),
+            dma(1),
+            dma(1),
             dma(3),
-            dma(3),
-            dma(4),
-            dma(4),
-            dma(4),
-            dma(4),
-            dma(5),
         ],
         compiler_params=pltpu.CompilerParams(
             collective_id=0, has_side_effects=True, vmem_limit_bytes=62 * MIB
@@ -571,7 +532,7 @@
             flops=4 * nodes * full * width, bytes_accessed=100 * MIB, transcendentals=0
         ),
         name="project",
-    )(latents, w_src, w_dst, send_tiles, norm, w_edge_out, w_node_in, w_node_out)
+    )(latents, w_src, w_dst, send_tiles, norm, w_node_in)
 
     crossing, norms = lax.optimization_barrier((w_node_in, norms))
     wi_far = lax.ppermute(crossing, "feat", [(0, 2), (2, 0), (1, 3), (3, 1)])

time: 130 us -> 131 us (level)
  Pallas kernels: 114 us -> 96.5 us
  between operations: 0.7 us -> 14.1 us
  waiting for transfers between devices: 9.76 us -> 15.4 us
    pallas_call x1, Pallas kernels: 74.8 us -> 60 us  [body(): pl.pallas_call(project_kernel, out_shape=(jax.ShapeDtypeStruct((table_row...]
    ppermute x1, waiting for transfers between devices: 9.76 us -> 14 us  [body(): wi_far = lax.ppermute(crossing, 'feat', [(0, 2), (2, 0), (1, 3), (3, 1)])]
    pallas_call x1, Pallas kernels: 12.2 us -> 9.77 us  [body(): pl.pallas_call(edge_kernel, out_shape=jax.ShapeDtypeStruct((nodes, width)...]
    unnamed x0 -> x2, waiting for transfers between devices: none -> 1.41 us
  transfers between devices with their start and end apart: 1 -> 3, of which waited for: 1 -> 1; matrix products, arithmetic and copies ran while one was open for 0% -> 1% of each run, Pallas kernels for 9% -> 53%
where the time goes in v4:
time: 131 us
  Pallas kernels  96.5 us (74%)
  waiting for transfers between devices  15.4 us (12%)
  between operations  14.1 us (11%)
  local copies, waits for them, and re-layouts  2.27 us (2%)
  other arithmetic  1.91 us (1%)
    pallas_call x1, Pallas kernels, body(): pl.pallas_call(project_kernel, out_shape=(jax.ShapeDtypeStruct((table_row...  60 us
    pallas_call x1, Pallas kernels, body(): pl.pallas_call(node_kernel, out_shape=jax.ShapeDtypeStruct((nodes, width)...  26.7 us
    ppermute x1, waiting for transfers between devices, body(): wi_far = lax.ppermute(crossing, 'feat', [(0, 2), (2, 0), (1, 3), (3, 1)])  14 us
    pallas_call x1, Pallas kernels, body(): pl.pallas_call(edge_kernel, out_shape=jax.ShapeDtypeStruct((nodes, width)...  9.77 us
  transfers between devices with their start and end apart: 3, of which 1 were waited for; matrix products, arithmetic and copies ran while one was open for 1% of the time, Pallas kernels for 53%

profile of v4, /device:TPU:0, one launch (start us, length us, event | category | flops | bytes accessed | tf_op | source)
XLA Modules:
  0.0 130.8 jit_solution(17895207939009102608)
XLA Ops:
  6.5 0.0 all-gather.5.cloned.1.call-start
  6.5 0.7 all-gather.5.cloned.1.call-update
  7.3 0.0 all-gather.7.cloned.1.call-start
  7.3 0.7 all-gather.7.cloned.1.call-update
  8.0 1.3 pad_maximum_fusion.norm_ref
  9.3 0.0 copy-start.2
  9.3 0.0 copy-start
  9.3 0.0 copy-start.1
  9.3 60.0 %project.1 = (bf16[6144,256]{1,0:T(8,128)(2,1)}, bf16[2048,256]{1,0:T(8,128)(2,1)}, bf16[512,1024]{1,0:T(8,128)(2,1)}, f32[4,2,256]{2,1,0:T(2,128)}, bf16[4,2048,256]{2,1,0:T(8,128)(2,1)}) custom-call(bf16[2048,256]{1,0:T(8,128)(2,1)} %lat_ref.1, bf16[1024,256]{1,0:T(8,128)(2,1)} %ws_hbm.1, bf16[1024,256]{1,0:T(8,128)(2,1)} %wd_hbm.1, s32[1,4,4]{2,1,0:T(4,128)} %st_ref.1, ...), custom_call_target="tpu_custom_call" | custom-call | flops 2147483648 | bytes 104857600 | tf_op jit(solution)/shard_map/project/pallas_call | solution.py:499
  69.3 0.0 copy-done.2
  69.3 0.6 collective-permute-start
  70.5 0.0 copy-done
  70.5 0.0 copy-done.1
  70.5 0.6 add_multiply_fusion.idx_ref
  71.2 9.8 %edges.1.summed_ref = bf16[2048,256]{1,0:T(8,128)(2,1)} custom-call(s32[96,128]{1,0:T(8,128)} %add_multiply_fusion.idx_ref, s32[1,96]{1,0:T(1,128)} %dst_tile_ref.1, s32[1]{0:T(128)S(6)} %copy.16.count_ref, s32[96,128]{1,0:T(8,128)} %off_ref.1, bf16[6144,256]{1,0:T(8,128)(2,1)} %get-tuple-element.12.table_hbm, bf16[2048,256]{1,0:T(8,128)(2,1)} %get-tuple-element.13.recv_hbm), custom_call_target="tpu_custom_call" | custom-call | flops 1610612736 | bytes 104857600 | tf_op jit(solution)/shard_map/edges/pallas_call | solution.py:541
  81.0 14.0 %collective-permute-done.wi_far = bf16[2048,256]{1,0:T(8,128)(2,1)} collective-permute-done((bf16[2048,256]{1,0:T(8,128)(2,1)S(1)}, bf16[2048,256]{1,0:T(8,128)(2,1)}, u32[]{:S(2)}, u32[]{:S(2)}) %collective-permute-start) | collective-permute-done | bytes 1048608 | tf_op jit(solution)/shard_map/ppermute | solution.py:538
  95.0 0.0 all-gather.5.cloned.1.call-done
  95.0 0.0 all-gather.7.cloned.1.call-done
  95.0 26.7 %nodes.1 = bf16[2048,256]{1,0:T(8,128)(2,1)} custom-call(bf16[2048,256]{1,0:T(8,128)(2,1)} %edges.1.summed_ref, bf16[512,1024]{1,0:T(8,128)(2,1)} %get-tuple-element.14.rows_hbm, bf16[4,256,1024]{2,1,0:T(8,128)(2,1)} %bitcast.6, bf16[4,2048,256]{2,1,0:T(8,128)(2,1)} %get-tuple-element.15.wi_hbm, bf16[2048,256]{1,0:T(8,128)(2,1)} %collective-permute-done.wi_far, ...), custom_call_target="tpu_custom_call" | custom-call | flops 4294967296 | bytes 62914560 | tf_op jit(solution)/shard_map/nodes/pallas_call | solution.py:563
  121.7 2.3 %copy.17 = bf16[2048,256]{1,0:T(8,128)(2,1)} copy(bf16[2048,256]{1,0:T(8,128)(2,1)} %nodes.1) | data formatting | bytes 2097152
Async XLA Ops:
  6.5 88.4 %all-gather.5.cloned.1.call-start = ((), (), s32[]{:S(2)}) async-start(), calls=%async_computation | async-start | bytes 2621440 | tf_op jit(solution)/shard_map/all_gather | solution.py:495
  7.3 87.7 %all-gather.7.cloned.1.call-start = ((), (), s32[]{:S(2)}) async-start(), calls=%async_computation.1 | async-start | bytes 2621440 | tf_op jit(solution)/shard_map/all_gather | solution.py:496
  9.3 60.0 %copy-start.2 = (bf16[2048,256]{1,0:T(8,128)(2,1)S(1)}, bf16[2048,256]{1,0:T(8,128)(2,1)}, u32[]{:S(2)}) copy-start(bf16[2048,256]{1,0:T(8,128)(2,1)} %wi_own.1) | copy-start | bytes 3145732
  9.3 61.2 %copy-start = (s32[96,128]{1,0:T(8,128)S(1)}, s32[96,128]{1,0:T(8,128)}, u32[]{:S(2)}) copy-start(s32[96,128]{1,0:T(8,128)} %param.24) | copy-start | bytes 147460
  9.3 61.3 %copy-start.1 = (s32[96,128]{1,0:T(8,128)S(1)}, s32[96,128]{1,0:T(8,128)}, u32[]{:S(2)}) copy-start(s32[96,128]{1,0:T(8,128)} %param.22) | copy-start | bytes 147460
  69.3 25.7 %collective-permute-start = (bf16[2048,256]{1,0:T(8,128)(2,1)S(1)}, bf16[2048,256]{1,0:T(8,128)(2,1)}, u32[]{:S(2)}, u32[]{:S(2)}) collective-permute-start(bf16[2048,256]{1,0:T(8,128)(2,1)S(1)} %copy-done.2), channel_id=1, source_target_pairs={{0,2},{2,0},{1,3},{3,1},{4,6},{6,4},{5,7},{7,5},{8,10},{10,8},{9,1... | collective-permute-start | bytes 3145736 | tf_op jit(solution)/shard_map/ppermute | solution.py:538
Sparse Core Ops, SparseCore 0:
  8.9 36.6 all-gather.4
  47.1 22.5 all-gather.6
